TPU v7x, 512 devices: a whole 4x4x16 slice. The times are simulated.
512 devices in a mesh: tgt: 16 (over x, y_lo, core), gz: 32 (over y_hi, z).
Axes of the slice: x: 4, y: 4 (y_hi: 2, y_lo: 2; y = y_hi * 2 + y_lo), z: 16, core: 2. Of those that a mesh axis runs over, the one named last changes fastest.
Arguments:
- flux: bfloat16 [512, 7808], P(('tgt', 'gz')), may hold values from -6 to 6
- ivar: bfloat16 [512, 7808], P(('tgt', 'gz')), may hold values from 0.099609375 to 10
- templates: bfloat16 [256, 10, 7808], P('gz', None, 'tgt'), may hold values from -0.08 to 0.08, as said below
- classes: int32 [512], P(('tgt', 'gz')), may hold values 0 or 1
Outputs:
- drop: float32 [512, 256], P(('tgt', 'gz'))
Inputs may be any that keep to these rules, and one draw needn't show every extreme that they name: `templates`: every weighted Gram matrix is positive definite.
All inputs are finite; a program needn't handle non-finite values. No bound on the sum of `classes` on one device may be relied on, other than what follows from the above.
Results may differ from a plain program's by a relative error of at most 0.0018.
Values may be sent and summed in bfloat16 or wider, within the bound.
No kernel may reach another device: no remote copies, remote signals or barrier semaphores. Data moves between devices by JAX's collectives and lax.ppermute only.
A program may use at most 64 MiB of HBM per device.

v0:
```python
import jax
import jax.numpy as jnp
from jax import lax
from jax.sharding import PartitionSpec as P


def pair_products(tmpl):
    wide = tmpl.astype(jnp.float32)
    count = wide.shape[1]
    pieces = [wide[:, k : k + 1, :] * wide[:, k:, :] for k in range(count)]
    return jnp.concatenate(pieces, axis=1).astype(jnp.bfloat16)


def solve_fit(gram, proj):
    count = proj.shape[-1]
    entries = jnp.moveaxis(gram, -1, 0)
    rights = jnp.moveaxis(proj, -1, 0)
    where = {}
    place = 0
    for k in range(count):
        for l in range(k, count):
            where[k, l] = place
            place = place + 1
    lower = {}
    for j in range(count):
        total = entries[where[j, j]]
        for m in range(j):
            total = total - lower[j, m] * lower[j, m]
        lower[j, j] = jnp.sqrt(total)
        for i in range(j + 1, count):
            value = entries[where[j, i]]
            for m in range(j):
                value = value - lower[i, m] * lower[j, m]
            lower[i, j] = value / lower[j, j]
    solved = []
    fit = jnp.zeros_like(rights[0])
    for i in range(count):
        value = rights[i]
        for m in range(i):
            value = value - lower[i, m] * solved[m]
        value = value / lower[i, i]
        solved.append(value)
        fit = fit + value * value
    return fit / count


def body(flux, ivar, templates, classes):
    weighted = (ivar.astype(jnp.float32) * flux.astype(jnp.float32)).astype(jnp.bfloat16)
    weight_rows, ivar_rows = (
        lax.all_gather(weighted, "gz", axis=0, tiled=True),
        lax.all_gather(ivar, "gz", axis=0, tiled=True),
    )
    slab = templates.shape[0]
    count = templates.shape[1]
    npairs = count * (count + 1) // 2
    nrows = weight_rows.shape[0]
    contract = (((1,), (1,)), ((), ()))
    piece = lax.all_gather(templates, "tgt", axis=2, tiled=True)
    width = piece.shape[2]
    pairs = pair_products(piece).reshape(slab * npairs, width)
    gram = lax.dot_general(ivar_rows, pairs, contract, preferred_element_type=jnp.float32)
    proj = lax.dot_general(
        weight_rows,
        piece.reshape(slab * count, width),
        contract,
        preferred_element_type=jnp.float32,
    )
    gram, proj = (gram, proj)
    gram = gram.reshape(nrows, slab, npairs)
    proj = proj.reshape(nrows, slab, count)
    fit_here = solve_fit(gram, proj)
    surface = lax.all_to_all(fit_here, "gz", split_axis=0, concat_axis=1, tiled=True)
    total_z = surface.shape[1]
    zindex = jnp.arange(total_z, dtype=jnp.int32)
    keep = (classes[:, None] == 1) | (zindex[None, :] < total_z * 3 // 10)
    return jnp.where(keep, surface, jnp.float32(0.0))


def solution(mesh):
    return jax.shard_map(
        body,
        mesh=mesh,
        in_specs=(
            P(("tgt", "gz"), None),
            P(("tgt", "gz"), None),
            P("gz", None, "tgt"),
            P(("tgt", "gz")),
        ),
        out_specs=P(("tgt", "gz"), None),
        check_vma=False,
    )
```

profile of v0, /device:TPU:6, one launch (start us, length us, event | category | flops | bytes accessed | tf_op | source)
XLA Modules:
  0.0 239.4 jit_solution(12519578691146313007)
XLA Ops:
  6.5 0.0 all-gather.4.cloned.1.call-start
  6.5 2.4 %copy.72 = bf16[8,10,488]{1,0,2:T(8,128)(2,1)} copy(bf16[8,10,488]{2,0,1:T(8,128)(2,1)} %param.6) | data formatting | bytes 156160 | tf_op args[2]
  9.0 0.0 all-gather.4.cloned.1.call-update
  9.0 0.8 convert_bitcast_fusion
  9.8 89.6 %all-gather = bf16[32,1,7808]{2,1,0:T(2,128)(2,1)S(1)} all-gather(bf16[1,1,7808]{2,1,0:T(2,128)(2,1)S(1)} %convert_bitcast_fusion), channel_id=1, replica_groups=mesh['tgt'=16,'gz'=32] {'gz'}, dimensions={0}, use_global_device_ids=true | all-gather | bytes 515328 | tf_op jit(solution)/shard_map/all_gather | solution.py:50
  99.4 76.7 %all-gather.1 = bf16[32,1,7808]{2,1,0:T(2,128)(2,1)S(1)} all-gather(bf16[1,1,7808]{2,1,0:T(2,128)(2,1)} %bitcast.450), channel_id=1, replica_groups=mesh['tgt'=16,'gz'=32] {'gz'}, dimensions={0}, use_global_device_ids=true | all-gather | bytes 515328 | tf_op jit(solution)/shard_map/all_gather | solution.py:51
  176.2 0.0 all-gather.4.cloned.1.call-done
  176.2 16.0 %copy.79 = bf16[8,10,7808]{2,0,1:T(8,128)(2,1)S(1)} copy(bf16[8,10,7808]{1,0,2:T(8,128)(2,1)} %all-gather.4.cloned.1.call-done) | data formatting | bytes 2498560 | tf_op jit(solution)/shard_map/all_gather | solution.py:58
  192.1 0.2 convert_element_type.20
  192.3 0.5 convolution_bitcast_fusion.1
  192.8 0.1 slice_bitcast_fusion
  193.0 0.2 fusion.4
  193.2 0.2 fusion.6
  193.4 0.2 fusion.7
  193.6 0.2 fusion.9
  193.7 0.1 fusion.10
  193.9 0.1 fusion.12
  194.0 0.1 fusion.13
  194.1 0.1 fusion.19
  194.2 0.1 fusion.20
  194.3 3.6 %copy.76 = bf16[8,55,7808]{2,1,0:T(8,128)(2,1)} copy(bf16[8,55,7808]{2,0,1:T(8,128)(2,1)S(1)} %fusion.22) | data formatting | bytes 13742080 | tf_op jit(solution)/shard_map/concatenate | solution.py:11
  197.9 8.3 %convert_element_type.21 = bf16[440,7808]{1,0:T(8,128)(2,1)} reshape(bf16[8,55,7808]{2,1,0:T(8,128)(2,1)} %copy.76) | data formatting | bytes 13742080 | tf_op jit(solution)/shard_map/convert_element_type | solution.py:11
  206.2 5.0 %convolution_bitcast_fusion = f32[32,440]{1,0:T(8,128)S(1)} fusion(bf16[440,7808]{1,0:T(8,128)(2,1)} %convert_element_type.21, bf16[32,1,7808]{2,1,0:T(2,128)(2,1)S(1)} %all-gather.1), kind=kOutput, calls=%fused_computation.13 | convolution fusion | flops 219873280 | bytes 7427072 | tf_op jit(solution)/shard_map/dot_general | solution.py:61
  211.1 0.1 reshape.2135
  211.2 0.2 copy.77
  211.4 0.1 fusion.36
  211.6 0.7 copy.78
  212.2 3.8 %all-to-all-start = ((f32[32,1,8]{2,1,0:T(1,128)}), f32[32,1,8]{2,1,0:T(1,128)S(1)}, u32[]{:S(2)}, u32[]{:S(2)}) async-start(f32[32,1,8]{2,1,0:T(1,128)} %copy.78), calls=%async_computation | async-start | bytes 32768 | tf_op jit(solution)/shard_map/all_to_all | solution.py:72
  216.7 14.0 %all-to-all-done = f32[32,1,8]{2,1,0:T(1,128)S(1)} async-done(((f32[32,1,8]{2,1,0:T(1,128)}), f32[32,1,8]{2,1,0:T(1,128)S(1)}, u32[]{:S(2)}, u32[]{:S(2)}) %all-to-all-start) | async-done | bytes 1056 | tf_op jit(solution)/shard_map/all_to_all | solution.py:72
  230.7 0.5 broadcast.36
  231.2 0.7 reduce.3
  231.9 0.1 all_to_all.11
  232.0 0.6 or_select_fusion
  (1 shorter events, 0.0 us)
Async XLA Ops:
  6.5 169.6 %all-gather.4.cloned.1.call-start = ((), (), s32[]{:S(2)}) async-start(), calls=%async_computation.1 | async-start | bytes 16990208 | tf_op jit(solution)/shard_map/all_gather | solution.py:58
  212.2 18.5 %all-to-all-start = ((f32[32,1,8]{2,1,0:T(1,128)}), f32[32,1,8]{2,1,0:T(1,128)S(1)}, u32[]{:S(2)}, u32[]{:S(2)}) async-start(f32[32,1,8]{2,1,0:T(1,128)} %copy.78), calls=%async_computation | async-start | bytes 32768 | tf_op jit(solution)/shard_map/all_to_all | solution.py:72
Sparse Core Ops, SparseCore 0:
  9.5 112.8 all-gather.3
where the time goes:
time: 240 us; the launch traced here: 239 us
  blocking collectives  166 us (69%)
  local copies, waits for them, and re-layouts  32 us (13%)
  between operations  14.2 us (6%)
  waiting for transfers between devices  14 us (6%)
  matrix products  5.43 us (2%)
  starting transfers between devices  3.81 us (2%)
  other arithmetic  3.69 us (2%)
    all_gather x1, blocking collectives, body(): lax.all_gather(weighted, 'gz', axis=0, tiled=True)  89.6 us
    all_gather x1, blocking collectives, body(): lax.all_gather(ivar, 'gz', axis=0, tiled=True)  76.7 us
    all_gather x1, local copies, waits for them, and re-layouts, body(): piece = lax.all_gather(templates, 'tgt', axis=2, tiled=True)  16 us
    all_to_all x1, waiting for transfers between devices, body(): lax.all_to_all(fit_here, 'gz', split_axis=0, concat_axis=1, tiled=True)  14 us
    convert_element_type x1, local copies, waits for them, and re-layouts, pair_products(): return jnp.concatenate(pieces, axis=1).astype(jnp.bfloat16)  8.28 us
    dot_general x1, matrix products, body(): lax.dot_general(ivar_rows, pairs, contract, preferred_element_type=jnp.fl...  4.95 us
  transfers between devices with their start and end apart: 2, of which 1 were waited for; matrix products, arithmetic and copies ran while one was open for 0% of the time, Pallas kernels for 0%

commit v1 on v0

v1 whole, which is shorter than its diff:
```python
import functools

import jax
import jax.numpy as jnp
from jax import lax
from jax.experimental import pallas as pl
from jax.experimental.pallas import tpu as pltpu
from jax.sharding import Mesh
from jax.sharding import PartitionSpec as P

BF16 = jnp.bfloat16
F32 = jnp.float32
LANES = 128
PAD = 512
TGT = ("x", "yl", "c")
GZ = ("yh", "z")
PLANE = ("x", "yl", "yh")
VMEM = pl.BlockSpec(memory_space=pltpu.VMEM)
SMEM = pl.BlockSpec(memory_space=pltpu.SMEM)
NT = (((1,), (1,)), ((), ()))


def pad16(n):
    return (n + 15) // 16 * 16


def strided(ref, start, size, stride):
    parts = [ref[j, pl.ds(start, size, stride=stride), :] for j in range(ref.shape[0])]
    return jnp.concatenate(parts, axis=1)


def prep_kernel(flux_ref, ivar_ref, tmpl_ref, rmsg_ref, tmsg_ref, rows, tmps):
    slab, count, width = tmpl_ref.shape
    chunks = rmsg_ref.shape[1] // 2
    rows[...] = jnp.zeros_like(rows)
    tmps[...] = jnp.zeros_like(tmps)
    ivar = ivar_ref[...].astype(F32)
    weighted = (ivar * flux_ref[...].astype(F32)).astype(BF16).astype(F32)
    for core in range(2):
        for which, value in enumerate((ivar, weighted)):
            for s in range(chunks):
                row = (core * 2 + which) * chunks + s
                start = (2 * s + core) * width
                rows[row : row + 1, 0:width] = value[:, start : start + width]
    rmsg_ref[...] = rows[...].reshape(rmsg_ref.shape).astype(BF16)
    step = pad16(count)
    for z in range(slab):
        value = tmpl_ref[z].astype(F32)
        for j in range(PAD // LANES):
            part = value[:, j * LANES : min((j + 1) * LANES, width)]
            tmps[j, z * step : z * step + count, 0 : part.shape[1]] = part
    for k in range(0, count, 2):
        both = [strided(tmps, k + i, slab, step) for i in range(2)]
        tile = jnp.concatenate(both, axis=0).astype(BF16)
        for copy in range(tmsg_ref.shape[0]):
            tmsg_ref[copy, k * slab : (k + 2) * slab, :] = tile


def gram_kernel(rows_ref, tmpl_ref, out_ref, rows, acc, *, slab, count):
    chunks = tmpl_ref.shape[0] // 2
    per = 2 * chunks
    nz = rows_ref.shape[0] // (2 * per)
    npairs = count * (count + 1) // 2
    for j in range(PAD // LANES):
        rows[j] = rows_ref[:, j * LANES : (j + 1) * LANES].astype(F32)
    for s in range(chunks):
        stat = []
        for which in range(2):
            cores = [
                strided(rows, core * per + which * chunks + s, nz, 2 * per)
                for core in range(2)
            ]
            stat.append(jnp.concatenate(cores, axis=0).astype(BF16))
        tk = []
        for k in range(count):
            halves = [
                tmpl_ref[2 * s + h, k * slab : (k + 1) * slab, :] for h in range(2)
            ]
            tk.append(jnp.concatenate(halves, axis=0))
        pairs = []
        for k in range(count):
            for l in range(k, count):
                pairs.append(
                    (tk[k].astype(F32) * tk[l].astype(F32)).astype(BF16)
                )
        gram = lax.dot_general(
            jnp.concatenate(pairs, axis=0), stat[0], NT, preferred_element_type=F32
        )
        proj = lax.dot_general(
            jnp.concatenate(tk, axis=0), stat[1], NT, preferred_element_type=F32
        )
        split = npairs * 2 * slab
        if s == 0:
            acc[0:split, :] = gram
            acc[split:, :] = proj
        else:
            acc[0:split, :] += gram
            acc[split:, :] += proj
    for e in range(npairs + count):
        for h in range(2):
            at = (2 * e + h) * slab
            out_ref[h, e * slab : (e + 1) * slab, :] = acc[at : at + slab, :]


def fit_kernel(part_ref, fit_ref, *, slab, count):
    npairs = count * (count + 1) // 2

    def entry(e):
        at = pl.ds(e * slab, slab)
        return part_ref[0, at, :] + part_ref[1, at, :]

    where = {}
    for k in range(count):
        for l in range(k, count):
            where[k, l] = len(where)
    lower = {}
    fit = None
    solved = []
    for j in range(count):
        total = entry(where[j, j])
        for m in range(j):
            total = total - lower[j, m] * lower[j, m]
        inv = lax.rsqrt(total)
        for i in range(j + 1, count):
            value = entry(where[j, i])
            for m in range(j):
                value = value - lower[i, m] * lower[j, m]
            lower[i, j] = value * inv
        value = entry(npairs + j)
        for m in range(j):
            value = value - lower[j, m] * solved[m]
        value = value * inv
        solved.append(value)
        fit = value * value if fit is None else fit + value * value
    fit_ref[...] = (fit / count).T


def drop_kernel(classes_ref, surface_ref, out_ref, *, galaxy_z):
    nsrc, slab = surface_ref.shape
    for i in range(nsrc):
        out_ref[:, i * slab : (i + 1) * slab] = surface_ref[i : i + 1, :]
    zindex = lax.broadcasted_iota(jnp.int32, out_ref.shape, 1)
    keep = (zindex < galaxy_z) | (classes_ref[0] == 1)
    out_ref[...] = jnp.where(keep, out_ref[...], 0.0)


def body(flux, ivar, templates, classes):
    slab, count, width = templates.shape
    entries = count * (count + 1) // 2 + count
    chunks = flux.shape[1] // width // 2
    rmsg, tmsg = pl.pallas_call(
        prep_kernel,
        out_shape=(
            jax.ShapeDtypeStruct((2, 2 * chunks, PAD), BF16),
            jax.ShapeDtypeStruct((2 * chunks, count * slab, PAD), BF16),
        ),
        in_specs=[VMEM] * 3,
        out_specs=(VMEM, VMEM),
        scratch_shapes=[
            pltpu.VMEM((4 * chunks, PAD), F32),
            pltpu.VMEM((PAD // LANES, slab * pad16(count), LANES), F32),
        ],
        name="prep",
    )(flux, ivar, templates)
    chip_rows = lax.all_gather(rmsg, "c", axis=0)
    mine = lax.dynamic_index_in_dim(chip_rows, lax.axis_index("c"), 1, keepdims=False)
    tmpl_all = lax.all_to_all(tmsg, PLANE, 0, 0, tiled=True)
    rows_all = lax.all_gather(mine, "z", axis=0)
    nz = rows_all.shape[0]
    part = pl.pallas_call(
        functools.partial(gram_kernel, slab=slab, count=count),
        out_shape=jax.ShapeDtypeStruct((2, entries * slab, 2 * nz), F32),
        in_specs=[VMEM] * 2,
        out_specs=VMEM,
        scratch_shapes=[
            pltpu.VMEM((PAD // LANES, nz * 4 * chunks, LANES), F32),
            pltpu.VMEM((entries * 2 * slab, 2 * nz), F32),
        ],
        compiler_params=pltpu.CompilerParams(vmem_limit_bytes=48 << 20),
        name="gram",
    )(rows_all.reshape(nz * 4 * chunks, PAD), tmpl_all)
    both = lax.all_to_all(part, "c", 0, 0, tiled=True)
    fit = pl.pallas_call(
        functools.partial(fit_kernel, slab=slab, count=count),
        out_shape=jax.ShapeDtypeStruct((2 * nz, slab), F32),
        in_specs=[VMEM],
        out_specs=VMEM,
        name="fit",
    )(both)
    surface = lax.all_to_all(fit, ("c", "z"), 0, 0, tiled=True)
    total_z = surface.shape[0] * slab
    return pl.pallas_call(
        functools.partial(drop_kernel, galaxy_z=total_z * 3 // 10),
        out_shape=jax.ShapeDtypeStruct((1, total_z), F32),
        in_specs=[SMEM, VMEM],
        out_specs=VMEM,
        name="drop",
    )(classes, surface)


def solution(mesh):
    fine = Mesh(mesh.devices.reshape(4, 2, 2, 2, 16), ("x", "yl", "c", "yh", "z"))
    return jax.shard_map(
        body,
        mesh=fine,
        in_specs=(
            P(TGT + GZ, None),
            P(TGT + GZ, None),
            P(GZ, None, TGT),
            P(TGT + GZ),
        ),
        out_specs=P(TGT + GZ, None),
        check_vma=False,
    )
```

time: 240 us -> 83.6 us (0.35)
  blocking collectives: 166 us -> 42.2 us
  local copies, waits for them, and re-layouts: 32 us -> 3.4 us
  between operations: 14.2 us -> 0.67 us
  starting transfers between devices: 3.81 us -> 16.3 us
  Pallas kernels: 0 us -> 8.2 us
  matrix products: 5.43 us -> 0 us
  other arithmetic: 3.69 us -> 0 us
  waiting for transfers between devices: 14 us -> 11.5 us
    all_gather x2, blocking collectives: 166 us -> 38.3 us  [the longest x1 36.5 us: body(): rows_all = lax.all_gather(mine, 'z', axis=0)]
    all_gather x1 -> x0, local copies, waits for them, and re-layouts: 16 us -> none  [body(): piece = lax.all_gather(templates, 'tgt', axis=2, tiled=True)]
    all_to_all x1 -> x2, starting transfers between devices: 3.8 us -> 16.3 us  [the longest x1 9.55 us: body(): tmpl_all = lax.all_to_all(tmsg, PLANE, 0, 0, tiled=True)]
    convert_element_type x1 -> x0, local copies, waits for them, and re-layouts: 8.28 us -> none  [pair_products(): return jnp.concatenate(pieces, axis=1).astype(jnp.bfloat16)]
    pallas_call x0 -> x4, Pallas kernels: none -> 8.2 us  [the longest x1 2.73 us: body(): pl.pallas_call(functools.partial(gram_kernel, slab=slab, count=count), ou...]
    dot_general x2 -> x0, matrix products: 5.43 us -> none  [the longest x1 4.95 us: body(): lax.dot_general(ivar_rows, pairs, contract, preferred_element_type=jnp.fl...]
    all_to_all x0 -> x1, blocking collectives: none -> 3.84 us  [body(): both = lax.all_to_all(part, 'c', 0, 0, tiled=True)]
    concatenate x1 -> x0, local copies, waits for them, and re-layouts: 3.58 us -> none  [pair_products(): return jnp.concatenate(pieces, axis=1).astype(jnp.bfloat16)]
where the time goes in v1:
time: 83.6 us; the launch traced here: 82.2 us
  blocking collectives  42.2 us (50%)
  starting transfers between devices  16.3 us (19%)
  waiting for transfers between devices  11.5 us (14%)
  Pallas kernels  8.2 us (10%)
  local copies, waits for them, and re-layouts  3.4 us (4%)
    all_gather x1, blocking collectives, body(): rows_all = lax.all_gather(mine, 'z', axis=0)  36.5 us
    all_to_all x1, waiting for transfers between devices, body(): surface = lax.all_to_all(fit, ('c', 'z'), 0, 0, tiled=True)  11.5 us
    all_to_all x1, starting transfers between devices, body(): tmpl_all = lax.all_to_all(tmsg, PLANE, 0, 0, tiled=True)  9.55 us
    all_to_all x1, starting transfers between devices, body(): surface = lax.all_to_all(fit, ('c', 'z'), 0, 0, tiled=True)  6.73 us
    all_to_all x1, blocking collectives, body(): both = lax.all_to_all(part, 'c', 0, 0, tiled=True)  3.84 us
    pallas_call x1, Pallas kernels, body(): pl.pallas_call(functools.partial(gram_kernel, slab=slab, count=count), ou...  2.73 us
    pallas_call x1, Pallas kernels, body(): pl.pallas_call(prep_kernel, out_shape=(jax.ShapeDtypeStruct((2, 2 * chunk...  2.27 us
    unnamed x5, local copies, waits for them, and re-layouts  2.18 us
  transfers between devices with their start and end apart: 2, of which 1 were waited for; matrix products, arithmetic and copies ran while one was open for 0% of the time, Pallas kernels for 0%

profile of v1, /device:TPU:6, one launch (start us, length us, event | category | flops | bytes accessed | tf_op | source)
XLA Modules:
  0.0 82.2 jit_solution(12315054727611304802)
XLA Ops:
  0.0 1.6 %copy.7.tmpl_ref = bf16[8,10,488]{2,1,0:T(8,128)(2,1)} copy(bf16[8,10,488]{2,0,1:T(8,128)(2,1)} %param.6) | data formatting | bytes 156160 | tf_op args[2]
  1.6 2.3 %prep.1 = (bf16[2,16,512]{2,1,0:T(8,128)(2,1)}, bf16[16,80,512]{2,1,0:T(8,128)(2,1)}) custom-call(bf16[1,7808]{1,0:T(2,128)(2,1)} %flux_ref.1, bf16[1,7808]{1,0:T(2,128)(2,1)} %ivar_ref.1, bf16[8,10,488]{2,1,0:T(8,128)(2,1)} %copy.7.tmpl_ref), custom_call_target="tpu_custom_call" | custom-call | tf_op jit(solution)/shard_map/prep/pallas_call | solution.py:151
  3.8 0.0 copy-start.1
  3.8 9.5 %all-to-all-start = ((bf16[16,80,512]{2,1,0:T(8,128)(2,1)}), bf16[16,80,512]{2,1,0:T(8,128)(2,1)S(1)}, u32[]{:S(2)}, u32[]{:S(2)}) async-start(bf16[16,80,512]{2,1,0:T(8,128)(2,1)} %get-tuple-element.8), calls=%async_computation | async-start | bytes 2621440 | tf_op jit(solution)/shard_map/all_to_all | solution.py:167
  13.4 0.0 copy-done.1
  13.4 1.9 %all-gather = bf16[4,16,512]{2,1,0:T(8,128)(2,1)S(1)} all-gather(bf16[2,16,512]{2,1,0:T(8,128)(2,1)S(1)} %copy-done.1), channel_id=2, replica_groups=mesh['x'=4,'yl'=2,'c'=2,'yh'=2,'z'=16] {'c'}, dimensions={0}, use_global_device_ids=true | all-gather | bytes 98304 | tf_op jit(solution)/shard_map/all_gather | solution.py:165
  15.3 36.5 %all-gather.1 = bf16[32,1,16,512]{3,2,1,0:T(8,128)(2,1)S(1)} all-gather(bf16[2,1,16,512]{3,2,1,0:T(8,128)(2,1)S(1)} %constant_dynamic-slice_fusion), channel_id=3, replica_groups=mesh['x'=4,'yl'=2,'c'=2,'yh'=2,'z'=16] {'z'}, dimensions={0}, use_global_device_ids=true | all-gather | bytes 557056 | tf_op jit(solution)/shard_map/all_gather | solution.py:168
  51.7 0.0 all-to-all-done.tmpl_ref
  51.7 2.7 %gram.1 = f32[2,520,32]{2,1,0:T(8,128)S(1)} custom-call(bf16[512,512]{1,0:T(8,128)(2,1)S(1)} %bitcast.6, bf16[16,80,512]{2,1,0:T(8,128)(2,1)S(1)} %all-to-all-done.tmpl_ref), custom_call_target="tpu_custom_call" | custom-call | tf_op jit(solution)/shard_map/gram/pallas_call | solution.py:170
  54.5 0.2 copy.8
  54.7 3.8 %all_to_all.21 = f32[2,520,32]{1,2,0:T(8,128)S(1)} all-to-all(f32[2,520,32]{1,2,0:T(8,128)S(1)} %copy.8), channel_id=1, replica_groups=mesh['x'=4,'yl'=2,'c'=2,'yh'=2,'z'=16] {'c'}, dimensions={0} | all-to-all | bytes 266240 | tf_op jit(solution)/shard_map/all_to_all | solution.py:182
  58.5 1.0 %copy.9.part_ref = f32[2,520,32]{2,1,0:T(8,128)} copy(f32[2,520,32]{1,2,0:T(8,128)S(1)} %all_to_all.21) | data formatting | bytes 266240 | tf_op jit(solution)/shard_map/all_to_all | solution.py:182
  59.5 1.8 %fit.1 = f32[32,8]{1,0:T(8,128)} custom-call(f32[2,520,32]{2,1,0:T(8,128)} %copy.9.part_ref), custom_call_target="tpu_custom_call" | custom-call | tf_op jit(solution)/shard_map/fit/pallas_call | solution.py:183
  61.3 6.7 %all-to-all-start.2 = ((f32[32,1,8]{2,1,0:T(1,128)}), f32[32,1,8]{2,1,0:T(1,128)S(1)}, u32[]{:S(2)}, u32[]{:S(2)}) async-start(f32[32,1,8]{2,1,0:T(1,128)} %bitcast.8), calls=%async_computation.2 | async-start | bytes 32768 | tf_op jit(solution)/shard_map/all_to_all | solution.py:190
  68.7 11.5 %all-to-all-done.2 = f32[32,1,8]{2,1,0:T(1,128)S(1)} async-done(((f32[32,1,8]{2,1,0:T(1,128)}), f32[32,1,8]{2,1,0:T(1,128)S(1)}, u32[]{:S(2)}, u32[]{:S(2)}) %all-to-all-start.2) | async-done | bytes 1056 | tf_op jit(solution)/shard_map/all_to_all | solution.py:190
  80.2 0.0 copy-start
  80.2 0.6 copy-done
  80.8 1.4 %drop.1 = f32[1,256]{1,0:T(1,128)} custom-call(s32[1]{0:T(128)S(6)} %copy.11.classes_ref, f32[32,8]{1,0:T(8,128)} %bitcast.9), custom_call_target="tpu_custom_call" | custom-call | tf_op jit(solution)/shard_map/drop/pallas_call | solution.py:192
  (1 shorter events, 0.0 us)
Async XLA Ops:
  3.8 9.6 %copy-start.1 = (bf16[2,16,512]{2,1,0:T(8,128)(2,1)S(1)}, bf16[2,16,512]{2,1,0:T(8,128)(2,1)}, u32[]{:S(2)}) copy-start(bf16[2,16,512]{2,1,0:T(8,128)(2,1)} %get-tuple-element.7) | copy-start | bytes 98308
  3.8 47.9 %all-to-all-start = ((bf16[16,80,512]{2,1,0:T(8,128)(2,1)}), bf16[16,80,512]{2,1,0:T(8,128)(2,1)S(1)}, u32[]{:S(2)}, u32[]{:S(2)}) async-start(bf16[16,80,512]{2,1,0:T(8,128)(2,1)} %get-tuple-element.8), calls=%async_computation | async-start | bytes 2621440 | tf_op jit(solution)/shard_map/all_to_all | solution.py:167
  61.3 18.9 %all-to-all-start.2 = ((f32[32,1,8]{2,1,0:T(1,128)}), f32[32,1,8]{2,1,0:T(1,128)S(1)}, u32[]{:S(2)}, u32[]{:S(2)}) async-start(f32[32,1,8]{2,1,0:T(1,128)} %bitcast.8), calls=%async_computation.2 | async-start | bytes 32768 | tf_op jit(solution)/shard_map/all_to_all | solution.py:190
  80.2 0.6 copy-start

commit v2 on v1

--- a/solution.py
+++ b/solution.py
@@ -20,20 +20,15 @@
 NT = (((1,), (1,)), ((), ()))
 
 
-def pad16(n):
-    return (n + 15) // 16 * 16
-
-
 def strided(ref, start, size, stride):
     parts = [ref[j, pl.ds(start, size, stride=stride), :] for j in range(ref.shape[0])]
     return jnp.concatenate(parts, axis=1)
 
 
-def prep_kernel(flux_ref, ivar_ref, tmpl_ref, rmsg_ref, tmsg_ref, rows, tmps):
-    slab, count, width = tmpl_ref.shape
+def prep_kernel(classes_ref, flux_ref, ivar_ref, tmpl_ref, rmsg_ref, tmsg_ref, keep_ref, rows, *, galaxy_z):
+    count, slab, width = tmpl_ref.shape
     chunks = rmsg_ref.shape[1] // 2
     rows[...] = jnp.zeros_like(rows)
-    tmps[...] = jnp.zeros_like(tmps)
     ivar = ivar_ref[...].astype(F32)
     weighted = (ivar * flux_ref[...].astype(F32)).astype(BF16).astype(F32)
     for core in range(2):
@@ -43,17 +38,12 @@
                 start = (2 * s + core) * width
                 rows[row : row + 1, 0:width] = value[:, start : start + width]
     rmsg_ref[...] = rows[...].reshape(rmsg_ref.shape).astype(BF16)
-    step = pad16(count)
-    for z in range(slab):
-        value = tmpl_ref[z].astype(F32)
-        for j in range(PAD // LANES):
-            part = value[:, j * LANES : min((j + 1) * LANES, width)]
-            tmps[j, z * step : z * step + count, 0 : part.shape[1]] = part
-    for k in range(0, count, 2):
-        both = [strided(tmps, k + i, slab, step) for i in range(2)]
-        tile = jnp.concatenate(both, axis=0).astype(BF16)
-        for copy in range(tmsg_ref.shape[0]):
-            tmsg_ref[copy, k * slab : (k + 2) * slab, :] = tile
+    zeros = jnp.zeros((count * slab, PAD - width), BF16)
+    tile = jnp.concatenate([tmpl_ref[...].reshape(count * slab, width), zeros], axis=1)
+    for copy in range(tmsg_ref.shape[0]):
+        tmsg_ref[copy] = tile
+    zindex = lax.broadcasted_iota(jnp.int32, keep_ref.shape, 1)
+    keep_ref[...] = jnp.where((zindex < galaxy_z) | (classes_ref[0] == 1), 1.0, 0.0)
 
 
 def gram_kernel(rows_ref, tmpl_ref, out_ref, rows, acc, *, slab, count):
@@ -96,18 +86,32 @@
         else:
             acc[0:split, :] += gram
             acc[split:, :] += proj
-    for e in range(npairs + count):
-        for h in range(2):
-            at = (2 * e + h) * slab
-            out_ref[h, e * slab : (e + 1) * slab, :] = acc[at : at + slab, :]
+    entries = npairs + count
+    ntarget = acc.shape[1]
+    fold = LANES // ntarget
+    for h in range(2):
+        for g in range(out_ref.shape[1] // slab):
+            parts = []
+            for e in range(g * fold, (g + 1) * fold):
+                at = (2 * min(e, entries - 1) + h) * slab
+                parts.append(acc[at : at + slab, :])
+            out_ref[h, g * slab : (g + 1) * slab, :] = jnp.concatenate(parts, axis=1)
 
 
 def fit_kernel(part_ref, fit_ref, *, slab, count):
     npairs = count * (count + 1) // 2
+    core = lax.axis_index("c")
+    ntarget = fit_ref.shape[0]
+    fold = LANES // ntarget
+    sums = {}
 
     def entry(e):
-        at = pl.ds(e * slab, slab)
-        return part_ref[0, at, :] + part_ref[1, at, :]
+        g = e // fold
+        if g not in sums:
+            at = pl.ds(g * slab, slab)
+            sums[g] = part_ref[0, core, at, :] + part_ref[1, core, at, :]
+        at = e % fold * ntarget
+        return sums[g][:, at : at + ntarget]
 
     where = {}
     for k in range(count):
@@ -135,33 +139,33 @@
     fit_ref[...] = (fit / count).T
 
 
-def drop_kernel(classes_ref, surface_ref, out_ref, *, galaxy_z):
+def drop_kernel(keep_ref, surface_ref, out_ref):
     nsrc, slab = surface_ref.shape
     for i in range(nsrc):
-        out_ref[:, i * slab : (i + 1) * slab] = surface_ref[i : i + 1, :]
-    zindex = lax.broadcasted_iota(jnp.int32, out_ref.shape, 1)
-    keep = (zindex < galaxy_z) | (classes_ref[0] == 1)
-    out_ref[...] = jnp.where(keep, out_ref[...], 0.0)
+        at = slice(i * slab, (i + 1) * slab)
+        value = surface_ref[i : i + 1, :]
+        out_ref[:, at] = jnp.where(keep_ref[:, at] > 0.0, value, 0.0)
 
 
 def body(flux, ivar, templates, classes):
     slab, count, width = templates.shape
     entries = count * (count + 1) // 2 + count
     chunks = flux.shape[1] // width // 2
-    rmsg, tmsg = pl.pallas_call(
-        prep_kernel,
+    total_z = lax.axis_size(GZ) * slab
+    fold = LANES // (2 * lax.axis_size("z"))
+    groups = -(-entries // fold)
+    rmsg, tmsg, keep = pl.pallas_call(
+        functools.partial(prep_kernel, galaxy_z=total_z * 3 // 10),
         out_shape=(
             jax.ShapeDtypeStruct((2, 2 * chunks, PAD), BF16),
             jax.ShapeDtypeStruct((2 * chunks, count * slab, PAD), BF16),
+            jax.ShapeDtypeStruct((1, total_z), F32),
         ),
-        in_specs=[VMEM] * 3,
-        out_specs=(VMEM, VMEM),
-        scratch_shapes=[
-            pltpu.VMEM((4 * chunks, PAD), F32),
-            pltpu.VMEM((PAD // LANES, slab * pad16(count), LANES), F32),
-        ],
+        in_specs=[SMEM] + [VMEM] * 3,
+        out_specs=(VMEM, VMEM, VMEM),
+        scratch_shapes=[pltpu.VMEM((4 * chunks, PAD), F32)],
         name="prep",
-    )(flux, ivar, templates)
+    )(classes, flux, ivar, jnp.transpose(templates, (1, 0, 2)))
     chip_rows = lax.all_gather(rmsg, "c", axis=0)
     mine = lax.dynamic_index_in_dim(chip_rows, lax.axis_index("c"), 1, keepdims=False)
     tmpl_all = lax.all_to_all(tmsg, PLANE, 0, 0, tiled=True)
@@ -169,7 +173,7 @@
     nz = rows_all.shape[0]
     part = pl.pallas_call(
         functools.partial(gram_kernel, slab=slab, count=count),
-        out_shape=jax.ShapeDtypeStruct((2, entries * slab, 2 * nz), F32),
+        out_shape=jax.ShapeDtypeStruct((2, groups * slab, LANES), F32),
         in_specs=[VMEM] * 2,
         out_specs=VMEM,
         scratch_shapes=[
@@ -179,7 +183,7 @@
         compiler_params=pltpu.CompilerParams(vmem_limit_bytes=48 << 20),
         name="gram",
     )(rows_all.reshape(nz * 4 * chunks, PAD), tmpl_all)
-    both = lax.all_to_all(part, "c", 0, 0, tiled=True)
+    both = lax.all_gather(part, "c", axis=0)
     fit = pl.pallas_call(
         functools.partial(fit_kernel, slab=slab, count=count),
         out_shape=jax.ShapeDtypeStruct((2 * nz, slab), F32),
@@ -188,14 +192,13 @@
         name="fit",
     )(both)
     surface = lax.all_to_all(fit, ("c", "z"), 0, 0, tiled=True)
-    total_z = surface.shape[0] * slab
     return pl.pallas_call(
-        functools.partial(drop_kernel, galaxy_z=total_z * 3 // 10),
+        drop_kernel,
         out_shape=jax.ShapeDtypeStruct((1, total_z), F32),
-        in_specs=[SMEM, VMEM],
+        in_specs=[VMEM, VMEM],
         out_specs=VMEM,
         name="drop",
-    )(classes, surface)
+    )(keep, surface)
 
 
 def solution(mesh):

time: 83.6 us -> 80.3 us (0.961)
  blocking collectives: 42.2 us -> 59.4 us
  waiting for transfers between devices: 11.5 us -> 0.01 us
  starting transfers between devices: 16.3 us -> 9.55 us
  local copies, waits for them, and re-layouts: 3.4 us -> 0.01 us
  Pallas kernels: 8.2 us -> 9.42 us
    all_to_all x1, blocking collectives: 3.84 us -> 19 us  [body(): surface = lax.all_to_all(fit, ('c', 'z'), 0, 0, tiled=True)]
    all_to_all x1 -> x0, waiting for transfers between devices: 11.5 us -> none  [body(): surface = lax.all_to_all(fit, ('c', 'z'), 0, 0, tiled=True)]
    all_to_all x1 -> x0, starting transfers between devices: 6.73 us -> none  [body(): surface = lax.all_to_all(fit, ('c', 'z'), 0, 0, tiled=True)]
    unnamed x5 -> x2, local copies, waits for them, and re-layouts: 2.18 us -> 0.01 us
    all_gather x0 -> x1, blocking collectives: none -> 2.14 us  [body(): both = lax.all_gather(part, 'c', axis=0)]
    pallas_call x1, Pallas kernels: 1.81 us -> 3.08 us  [body(): pl.pallas_call(functools.partial(fit_kernel, slab=slab, count=count), out...]
    all_to_all x1 -> x0, local copies, waits for them, and re-layouts: 1.01 us -> none  [body(): both = lax.all_to_all(part, 'c', 0, 0, tiled=True)]
  transfers between devices with their start and end apart: 2 -> 1, of which waited for: 1 -> 0; matrix products, arithmetic and copies ran while one was open for 0% -> 0% of each run, Pallas kernels for 0% -> 0%
where the time goes in v2:
time: 80.3 us; the launch traced here: 79.1 us
  blocking collectives  59.4 us (74%)
  starting transfers between devices  9.55 us (12%)
  Pallas kernels  9.42 us (12%)
    all_gather x1, blocking collectives, body(): rows_all = lax.all_gather(mine, 'z', axis=0)  36.5 us
    all_to_all x1, blocking collectives, body(): surface = lax.all_to_all(fit, ('c', 'z'), 0, 0, tiled=True)  19 us
    all_to_all x1, starting transfers between devices, body(): tmpl_all = lax.all_to_all(tmsg, PLANE, 0, 0, tiled=True)  9.55 us
    pallas_call x1, Pallas kernels, body(): pl.pallas_call(functools.partial(fit_kernel, slab=slab, count=count), out...  3.08 us
    pallas_call x1, Pallas kernels, body(): pl.pallas_call(functools.partial(gram_kernel, slab=slab, count=count), ou...  2.78 us
    pallas_call x1, Pallas kernels, body(): pl.pallas_call(functools.partial(prep_kernel, galaxy_z=total_z * 3 // 10)...  2.17 us
    all_gather x1, blocking collectives, body(): both = lax.all_gather(part, 'c', axis=0)  2.14 us
    all_gather x1, blocking collectives, body(): chip_rows = lax.all_gather(rmsg, 'c', axis=0)  1.85 us
  transfers between devices with their start and end apart: 1, of which 0 were waited for; matrix products, arithmetic and copies ran while one was open for 0% of the time, Pallas kernels for 0%

profile of v2, /device:TPU:6, one launch (start us, length us, event | category | flops | bytes accessed | tf_op | source)
XLA Modules:
  0.0 79.1 jit_solution(2333411922763231410)
XLA Ops:
  0.7 2.2 %prep.1 = (bf16[2,16,512]{2,1,0:T(8,128)(2,1)}, bf16[16,80,512]{2,1,0:T(8,128)(2,1)}, f32[1,256]{1,0:T(1,128)}) custom-call(s32[1]{0:T(128)S(6)} %copy.7.classes_ref, bf16[1,7808]{1,0:T(2,128)(2,1)} %flux_ref.1, bf16[1,7808]{1,0:T(2,128)(2,1)} %ivar_ref.1, bf16[10,8,488]{2,1,0:T(8,128)(2,1)} %bitcast.11), custom_call_target="tpu_custom_call" | custom-call | tf_op jit(solution)/shard_map/prep/pallas_call | solution.py:157
  2.8 0.0 copy-start
  2.8 9.5 %all-to-all-start = ((bf16[16,80,512]{2,1,0:T(8,128)(2,1)}), bf16[16,80,512]{2,1,0:T(8,128)(2,1)S(1)}, u32[]{:S(2)}, u32[]{:S(2)}) async-start(bf16[16,80,512]{2,1,0:T(8,128)(2,1)} %get-tuple-element.10), calls=%async_computation | async-start | bytes 2621440 | tf_op jit(solution)/shard_map/all_to_all | solution.py:171
  12.4 0.0 copy-done
  12.4 1.9 %all-gather = bf16[4,16,512]{2,1,0:T(8,128)(2,1)S(1)} all-gather(bf16[2,16,512]{2,1,0:T(8,128)(2,1)S(1)} %copy-done), channel_id=2, replica_groups=mesh['x'=4,'yl'=2,'c'=2,'yh'=2,'z'=16] {'c'}, dimensions={0}, use_global_device_ids=true | all-gather | bytes 98304 | tf_op jit(solution)/shard_map/all_gather | solution.py:169
  14.2 36.5 %all-gather.1 = bf16[32,1,16,512]{3,2,1,0:T(8,128)(2,1)S(1)} all-gather(bf16[2,1,16,512]{3,2,1,0:T(8,128)(2,1)S(1)} %constant_dynamic-slice_fusion), channel_id=3, replica_groups=mesh['x'=4,'yl'=2,'c'=2,'yh'=2,'z'=16] {'z'}, dimensions={0}, use_global_device_ids=true | all-gather | bytes 557056 | tf_op jit(solution)/shard_map/all_gather | solution.py:172
  50.7 0.0 all-to-all-done.tmpl_ref
  50.7 2.8 %gram.1 = f32[2,136,128]{2,1,0:T(8,128)S(1)} custom-call(bf16[512,512]{1,0:T(8,128)(2,1)S(1)} %bitcast.8, bf16[16,80,512]{2,1,0:T(8,128)(2,1)S(1)} %all-to-all-done.tmpl_ref), custom_call_target="tpu_custom_call" | custom-call | tf_op jit(solution)/shard_map/gram/pallas_call | solution.py:174
  53.5 2.1 %all-gather.2 = f32[4,136,128]{2,1,0:T(8,128)} all-gather(f32[2,136,128]{2,1,0:T(8,128)S(1)} %gram.1), channel_id=4, replica_groups=mesh['x'=4,'yl'=2,'c'=2,'yh'=2,'z'=16] {'c'}, dimensions={0}, use_global_device_ids=true | all-gather | bytes 417792 | tf_op jit(solution)/shard_map/all_gather | solution.py:186
  55.6 3.1 %fit.1 = f32[32,8]{1,0:T(8,128)} custom-call(f32[2,2,136,128]{3,2,1,0:T(8,128)} %bitcast.9), custom_call_target="tpu_custom_call" | custom-call | tf_op jit(solution)/shard_map/fit/pallas_call | solution.py:187
  58.7 19.0 %all_to_all.16 = f32[32,1,8]{2,1,0:T(1,128)} all-to-all(f32[32,1,8]{2,1,0:T(1,128)} %bitcast.12), channel_id=1, replica_groups=mesh['x'=4,'yl'=2,'c'=2,'yh'=2,'z'=16] {'c','z'}, dimensions={0} | all-to-all | bytes 2048 | tf_op jit(solution)/shard_map/all_to_all | solution.py:194
  77.7 1.4 %drop.1 = f32[1,256]{1,0:T(1,128)} custom-call(f32[1,256]{1,0:T(1,128)} %get-tuple-element.8.keep_ref, f32[32,8]{1,0:T(8,128)} %bitcast.13), custom_call_target="tpu_custom_call" | custom-call | tf_op jit(solution)/shard_map/drop/pallas_call | solution.py:195
  (1 shorter events, 0.0 us)
Async XLA Ops:
  2.8 9.6 %copy-start = (bf16[2,16,512]{2,1,0:T(8,128)(2,1)S(1)}, bf16[2,16,512]{2,1,0:T(8,128)(2,1)}, u32[]{:S(2)}) copy-start(bf16[2,16,512]{2,1,0:T(8,128)(2,1)} %get-tuple-element.9) | copy-start | bytes 98308
  2.8 47.9 %all-to-all-start = ((bf16[16,80,512]{2,1,0:T(8,128)(2,1)}), bf16[16,80,512]{2,1,0:T(8,128)(2,1)S(1)}, u32[]{:S(2)}, u32[]{:S(2)}) async-start(bf16[16,80,512]{2,1,0:T(8,128)(2,1)} %get-tuple-element.10), calls=%async_computation | async-start | bytes 2621440 | tf_op jit(solution)/shard_map/all_to_all | solution.py:171

commit v3 on v2

--- a/solution.py
+++ b/solution.py
@@ -18,6 +18,14 @@
 VMEM = pl.BlockSpec(memory_space=pltpu.VMEM)
 SMEM = pl.BlockSpec(memory_space=pltpu.SMEM)
 NT = (((1,), (1,)), ((), ()))
+
+
+def in_hbm(x):
+    return pltpu.with_memory_space_constraint(x, pltpu.HBM)
+
+
+def in_vmem(x):
+    return pltpu.with_memory_space_constraint(x, pltpu.VMEM)
 
 
 def strided(ref, start, size, stride):
@@ -157,15 +165,16 @@
     rmsg, tmsg, keep = pl.pallas_call(
         functools.partial(prep_kernel, galaxy_z=total_z * 3 // 10),
         out_shape=(
-            jax.ShapeDtypeStruct((2, 2 * chunks, PAD), BF16),
-            jax.ShapeDtypeStruct((2 * chunks, count * slab, PAD), BF16),
+            pltpu.VMEM((2, 2 * chunks, PAD), BF16),
+            pltpu.VMEM((2 * chunks, count * slab, PAD), BF16),
             jax.ShapeDtypeStruct((1, total_z), F32),
         ),
         in_specs=[SMEM] + [VMEM] * 3,
         out_specs=(VMEM, VMEM, VMEM),
         scratch_shapes=[pltpu.VMEM((4 * chunks, PAD), F32)],
+        compiler_params=pltpu.CompilerParams(vmem_limit_bytes=8 << 20),
         name="prep",
-    )(classes, flux, ivar, jnp.transpose(templates, (1, 0, 2)))
+    )(classes, in_hbm(flux), in_hbm(ivar), in_hbm(jnp.transpose(templates, (1, 0, 2))))
     chip_rows = lax.all_gather(rmsg, "c", axis=0)
     mine = lax.dynamic_index_in_dim(chip_rows, lax.axis_index("c"), 1, keepdims=False)
     tmpl_all = lax.all_to_all(tmsg, PLANE, 0, 0, tiled=True)
@@ -173,32 +182,34 @@
     nz = rows_all.shape[0]
     part = pl.pallas_call(
         functools.partial(gram_kernel, slab=slab, count=count),
-        out_shape=jax.ShapeDtypeStruct((2, groups * slab, LANES), F32),
+        out_shape=pltpu.VMEM((2, groups * slab, LANES), F32),
         in_specs=[VMEM] * 2,
         out_specs=VMEM,
         scratch_shapes=[
             pltpu.VMEM((PAD // LANES, nz * 4 * chunks, LANES), F32),
             pltpu.VMEM((entries * 2 * slab, 2 * nz), F32),
         ],
-        compiler_params=pltpu.CompilerParams(vmem_limit_bytes=48 << 20),
+        compiler_params=pltpu.CompilerParams(vmem_limit_bytes=16 << 20),
         name="gram",
     )(rows_all.reshape(nz * 4 * chunks, PAD), tmpl_all)
     both = lax.all_gather(part, "c", axis=0)
     fit = pl.pallas_call(
         functools.partial(fit_kernel, slab=slab, count=count),
-        out_shape=jax.ShapeDtypeStruct((2 * nz, slab), F32),
+        out_shape=pltpu.VMEM((2 * nz, slab), F32),
         in_specs=[VMEM],
         out_specs=VMEM,
+        compiler_params=pltpu.CompilerParams(vmem_limit_bytes=4 << 20),
         name="fit",
-    )(both)
+    )(in_vmem(both))
     surface = lax.all_to_all(fit, ("c", "z"), 0, 0, tiled=True)
     return pl.pallas_call(
         drop_kernel,
         out_shape=jax.ShapeDtypeStruct((1, total_z), F32),
         in_specs=[VMEM, VMEM],
         out_specs=VMEM,
+        compiler_params=pltpu.CompilerParams(vmem_limit_bytes=4 << 20),
         name="drop",
-    )(keep, surface)
+    )(in_vmem(keep), in_vmem(surface))
 
 
 def solution(mesh):

time: 80.3 us -> 77.4 us (0.964)
  Pallas kernels: 9.42 us -> 7.13 us
    pallas_call x1, Pallas kernels: 3.08 us -> 1.52 us  [body(): pl.pallas_call(functools.partial(fit_kernel, slab=slab, count=count), out...]
where the time goes in v3:
time: 77.4 us; the launch traced here: 76.2 us
  blocking collectives  59 us (76%)
  starting transfers between devices  9.42 us (12%)
  Pallas kernels  7.13 us (9%)
    all_gather x1, blocking collectives, body(): rows_all = lax.all_gather(mine, 'z', axis=0)  36.5 us
    all_to_all x1, blocking collectives, body(): surface = lax.all_to_all(fit, ('c', 'z'), 0, 0, tiled=True)  18.7 us
    all_to_all x1, starting transfers between devices, body(): tmpl_all = lax.all_to_all(tmsg, PLANE, 0, 0, tiled=True)  9.42 us
    pallas_call x1, Pallas kernels, body(): pl.pallas_call(functools.partial(gram_kernel, slab=slab, count=count), ou...  2.79 us
    pallas_call x1, Pallas kernels, body(): pl.pallas_call(functools.partial(prep_kernel, galaxy_z=total_z * 3 // 10)...  2.16 us
    all_gather x1, blocking collectives, body(): both = lax.all_gather(part, 'c', axis=0)  2.01 us
    all_gather x1, blocking collectives, body(): chip_rows = lax.all_gather(rmsg, 'c', axis=0)  1.84 us
  transfers between devices with their start and end apart: 1, of which 0 were waited for; matrix products, arithmetic and copies ran while one was open for 0% of the time, Pallas kernels for 0%

profile of v3, /device:TPU:6, one launch (start us, length us, event | category | flops | bytes accessed | tf_op | source)
XLA Modules:
  0.0 76.2 jit_solution(12228125705605971071)
XLA Ops:
  0.7 2.2 %prep.1 = (bf16[2,16,512]{2,1,0:T(8,128)(2,1)S(1)}, bf16[16,80,512]{2,1,0:T(8,128)(2,1)}, f32[1,256]{1,0:T(1,128)S(1)}) custom-call(s32[1]{0:T(128)S(6)} %copy.7.classes_ref, bf16[1,7808]{1,0:T(2,128)(2,1)} %flux_ref.1, bf16[1,7808]{1,0:T(2,128)(2,1)} %ivar_ref.1, bf16[10,8,488]{2,1,0:T(8,128)(2,1)} %bitcast.13), custom_call_target="tpu_custom_call" | custom-call | tf_op jit(solution)/shard_map/prep/pallas_call | solution.py:165
  2.8 9.4 %all-to-all-start = ((bf16[16,80,512]{2,1,0:T(8,128)(2,1)}), bf16[16,80,512]{2,1,0:T(8,128)(2,1)S(1)}, u32[]{:S(2)}, u32[]{:S(2)}) async-start(bf16[16,80,512]{2,1,0:T(8,128)(2,1)} %get-tuple-element.10), calls=%async_computation | async-start | bytes 2621440 | tf_op jit(solution)/shard_map/all_to_all | solution.py:180
  12.2 1.8 %all-gather = bf16[4,16,512]{2,1,0:T(8,128)(2,1)S(1)} all-gather(bf16[2,16,512]{2,1,0:T(8,128)(2,1)S(1)} %get-tuple-element.9), channel_id=2, replica_groups=mesh['x'=4,'yl'=2,'c'=2,'yh'=2,'z'=16] {'c'}, dimensions={0}, use_global_device_ids=true | all-gather | bytes 98304 | tf_op jit(solution)/shard_map/all_gather | solution.py:178
  14.1 36.5 %all-gather.1 = bf16[32,1,16,512]{3,2,1,0:T(8,128)(2,1)S(1)} all-gather(bf16[2,1,16,512]{3,2,1,0:T(8,128)(2,1)S(1)} %constant_dynamic-slice_fusion), channel_id=3, replica_groups=mesh['x'=4,'yl'=2,'c'=2,'yh'=2,'z'=16] {'z'}, dimensions={0}, use_global_device_ids=true | all-gather | bytes 557056 | tf_op jit(solution)/shard_map/all_gather | solution.py:181
  50.5 0.0 all-to-all-done.tmpl_ref
  50.5 2.8 %gram.1 = f32[2,136,128]{2,1,0:T(8,128)S(1)} custom-call(bf16[512,512]{1,0:T(8,128)(2,1)S(1)} %bitcast.8, bf16[16,80,512]{2,1,0:T(8,128)(2,1)S(1)} %all-to-all-done.tmpl_ref), custom_call_target="tpu_custom_call" | custom-call | tf_op jit(solution)/shard_map/gram/pallas_call | solution.py:183
  53.3 2.0 %all-gather.2 = f32[4,136,128]{2,1,0:T(8,128)S(1)} all-gather(f32[2,136,128]{2,1,0:T(8,128)S(1)} %gram.1), channel_id=4, replica_groups=mesh['x'=4,'yl'=2,'c'=2,'yh'=2,'z'=16] {'c'}, dimensions={0}, use_global_device_ids=true | all-gather | bytes 417792 | tf_op jit(solution)/shard_map/all_gather | solution.py:195
  55.3 1.5 %fit.1 = f32[32,8]{1,0:T(8,128)S(1)} custom-call(f32[2,2,136,128]{3,2,1,0:T(8,128)S(1)} %bitcast.9), custom_call_target="tpu_custom_call" | custom-call | tf_op jit(solution)/shard_map/fit/pallas_call | solution.py:196
  56.9 18.7 %all_to_all.16 = f32[32,1,8]{2,1,0:T(1,128)S(1)} all-to-all(f32[32,1,8]{2,1,0:T(1,128)S(1)} %bitcast.10), channel_id=1, replica_groups=mesh['x'=4,'yl'=2,'c'=2,'yh'=2,'z'=16] {'c','z'}, dimensions={0} | all-to-all | bytes 2048 | tf_op jit(solution)/shard_map/all_to_all | solution.py:204
  75.5 0.7 drop.1
  (1 shorter events, 0.0 us)
Async XLA Ops:
  2.8 47.7 %all-to-all-start = ((bf16[16,80,512]{2,1,0:T(8,128)(2,1)}), bf16[16,80,512]{2,1,0:T(8,128)(2,1)S(1)}, u32[]{:S(2)}, u32[]{:S(2)}) async-start(bf16[16,80,512]{2,1,0:T(8,128)(2,1)} %get-tuple-element.10), calls=%async_computation | async-start | bytes 2621440 | tf_op jit(solution)/shard_map/all_to_all | solution.py:180

commit v4 on v3

--- a/solution.py
+++ b/solution.py
@@ -35,8 +35,7 @@
 
 def prep_kernel(classes_ref, flux_ref, ivar_ref, tmpl_ref, rmsg_ref, tmsg_ref, keep_ref, rows, *, galaxy_z):
     count, slab, width = tmpl_ref.shape
-    chunks = rmsg_ref.shape[1] // 2
-    rows[...] = jnp.zeros_like(rows)
+    chunks = rmsg_ref.shape[0] // 4
     ivar = ivar_ref[...].astype(F32)
     weighted = (ivar * flux_ref[...].astype(F32)).astype(BF16).astype(F32)
     for core in range(2):
@@ -44,8 +43,8 @@
             for s in range(chunks):
                 row = (core * 2 + which) * chunks + s
                 start = (2 * s + core) * width
-                rows[row : row + 1, 0:width] = value[:, start : start + width]
-    rmsg_ref[...] = rows[...].reshape(rmsg_ref.shape).astype(BF16)
+                rows[row : row + 1, :] = value[:, start : start + width]
+    rmsg_ref[...] = rows[...].astype(BF16)
     zeros = jnp.zeros((count * slab, PAD - width), BF16)
     tile = jnp.concatenate([tmpl_ref[...].reshape(count * slab, width), zeros], axis=1)
     for copy in range(tmsg_ref.shape[0]):
@@ -57,18 +56,24 @@
 def gram_kernel(rows_ref, tmpl_ref, out_ref, rows, acc, *, slab, count):
     chunks = tmpl_ref.shape[0] // 2
     per = 2 * chunks
-    nz = rows_ref.shape[0] // (2 * per)
+    nz, width = rows_ref.shape[1], rows_ref.shape[3]
     npairs = count * (count + 1) // 2
-    for j in range(PAD // LANES):
-        rows[j] = rows_ref[:, j * LANES : (j + 1) * LANES].astype(F32)
+    core, z = lax.axis_index("c"), lax.axis_index("z")
+    last = PAD // LANES - 1
+    rows[last] = jnp.zeros_like(rows[last])
+    for j in range(2):
+        for other in range(nz):
+            block = rows_ref[j, other, pl.ds(core * per, per), :].astype(F32)
+            owner = lax.rem(j + z + other, 2)
+            at = pl.ds((owner * nz + other) * per, per)
+            for i in range(last + 1):
+                part = block[:, i * LANES : min((i + 1) * LANES, width)]
+                rows[i, at, 0 : part.shape[1]] = part
     for s in range(chunks):
         stat = []
         for which in range(2):
-            cores = [
-                strided(rows, core * per + which * chunks + s, nz, 2 * per)
-                for core in range(2)
-            ]
-            stat.append(jnp.concatenate(cores, axis=0).astype(BF16))
+            value = strided(rows, which * chunks + s, 2 * nz, per)
+            stat.append(value.astype(BF16))
         tk = []
         for k in range(count):
             halves = [
@@ -165,33 +170,33 @@
     rmsg, tmsg, keep = pl.pallas_call(
         functools.partial(prep_kernel, galaxy_z=total_z * 3 // 10),
         out_shape=(
-            pltpu.VMEM((2, 2 * chunks, PAD), BF16),
+            pltpu.VMEM((2 * 2 * chunks, width), BF16),
             pltpu.VMEM((2 * chunks, count * slab, PAD), BF16),
             jax.ShapeDtypeStruct((1, total_z), F32),
         ),
         in_specs=[SMEM] + [VMEM] * 3,
         out_specs=(VMEM, VMEM, VMEM),
-        scratch_shapes=[pltpu.VMEM((4 * chunks, PAD), F32)],
+        scratch_shapes=[pltpu.VMEM((4 * chunks, width), F32)],
         compiler_params=pltpu.CompilerParams(vmem_limit_bytes=8 << 20),
         name="prep",
     )(classes, in_hbm(flux), in_hbm(ivar), in_hbm(jnp.transpose(templates, (1, 0, 2))))
-    chip_rows = lax.all_gather(rmsg, "c", axis=0)
-    mine = lax.dynamic_index_in_dim(chip_rows, lax.axis_index("c"), 1, keepdims=False)
     tmpl_all = lax.all_to_all(tmsg, PLANE, 0, 0, tiled=True)
-    rows_all = lax.all_gather(mine, "z", axis=0)
-    nz = rows_all.shape[0]
+    nz = lax.axis_size("z")
+    rings = [[(g + z) % 2 * nz + z for z in range(nz)] for g in range(2)]
+    ring_rows = lax.all_gather(rmsg, ("c", "z"), axis=0, axis_index_groups=rings)
+    rows_all = lax.all_gather(ring_rows, "c", axis=0)
     part = pl.pallas_call(
         functools.partial(gram_kernel, slab=slab, count=count),
         out_shape=pltpu.VMEM((2, groups * slab, LANES), F32),
         in_specs=[VMEM] * 2,
         out_specs=VMEM,
         scratch_shapes=[
-            pltpu.VMEM((PAD // LANES, nz * 4 * chunks, LANES), F32),
+            pltpu.VMEM((PAD // LANES, 2 * nz * 2 * chunks, LANES), F32),
             pltpu.VMEM((entries * 2 * slab, 2 * nz), F32),
         ],
         compiler_params=pltpu.CompilerParams(vmem_limit_bytes=16 << 20),
         name="gram",
-    )(rows_all.reshape(nz * 4 * chunks, PAD), tmpl_all)
+    )(in_vmem(rows_all), tmpl_all)
     both = lax.all_gather(part, "c", axis=0)
     fit = pl.pallas_call(
         functools.partial(fit_kernel, slab=slab, count=count),

time: 77.4 us -> 75.3 us (0.973)
  blocking collectives: 59 us -> 56.8 us
    all_gather x2, blocking collectives: 38.3 us -> 35.7 us  [the longest x1 33.1 us: body(): lax.all_gather(rmsg, ('c', 'z'), axis=0, axis_index_groups=rings)]
where the time goes in v4:
time: 75.3 us; the launch traced here: 73.9 us
  blocking collectives  56.8 us (75%)
  starting transfers between devices  9.42 us (13%)
  Pallas kernels  7.03 us (9%)
    all_gather x1, blocking collectives, body(): lax.all_gather(rmsg, ('c', 'z'), axis=0, axis_index_groups=rings)  33.1 us
    all_to_all x1, blocking collectives, body(): surface = lax.all_to_all(fit, ('c', 'z'), 0, 0, tiled=True)  19.1 us
    all_to_all x1, starting transfers between devices, body(): tmpl_all = lax.all_to_all(tmsg, PLANE, 0, 0, tiled=True)  9.42 us
    pallas_call x1, Pallas kernels, body(): pl.pallas_call(functools.partial(gram_kernel, slab=slab, count=count), ou...  2.68 us
    all_gather x1, blocking collectives, body(): rows_all = lax.all_gather(ring_rows, 'c', axis=0)  2.57 us
    pallas_call x1, Pallas kernels, body(): pl.pallas_call(functools.partial(prep_kernel, galaxy_z=total_z * 3 // 10)...  2.17 us
    all_gather x1, blocking collectives, body(): both = lax.all_gather(part, 'c', axis=0)  2.02 us
    pallas_call x1, Pallas kernels, body(): pl.pallas_call(functools.partial(fit_kernel, slab=slab, count=count), out...  1.52 us
  transfers between devices with their start and end apart: 1, of which 0 were waited for; matrix products, arithmetic and copies ran while one was open for 0% of the time, Pallas kernels for 0%

profile of v4, /device:TPU:6, one launch (start us, length us, event | category | flops | bytes accessed | tf_op | source)
XLA Modules:
  0.0 73.9 jit_solution(14246044904732888677)
XLA Ops:
  0.7 2.2 %prep.1 = (bf16[32,488]{1,0:T(8,128)(2,1)S(1)}, bf16[16,80,512]{2,1,0:T(8,128)(2,1)}, f32[1,256]{1,0:T(1,128)S(1)}) custom-call(s32[1]{0:T(128)S(6)} %copy.6.classes_ref, bf16[1,7808]{1,0:T(2,128)(2,1)} %flux_ref.1, bf16[1,7808]{1,0:T(2,128)(2,1)} %ivar_ref.1, bf16[10,8,488]{2,1,0:T(8,128)(2,1)} %bitcast.13), custom_call_target="tpu_custom_call" | custom-call | tf_op jit(solution)/shard_map/prep/pallas_call | solution.py:170
  2.8 9.4 %all-to-all-start = ((bf16[16,80,512]{2,1,0:T(8,128)(2,1)}), bf16[16,80,512]{2,1,0:T(8,128)(2,1)S(1)}, u32[]{:S(2)}, u32[]{:S(2)}) async-start(bf16[16,80,512]{2,1,0:T(8,128)(2,1)} %get-tuple-element.10), calls=%async_computation | async-start | bytes 2621440 | tf_op jit(solution)/shard_map/all_to_all | solution.py:183
  12.2 33.1 %all-gather = bf16[512,488]{1,0:T(8,128)(2,1)S(1)} all-gather(bf16[32,488]{1,0:T(8,128)(2,1)S(1)} %get-tuple-element.9), channel_id=2, replica_groups={{0,33,2,35,4,37,6,39,8,41,10,43,12,45,14,47},{32,1,34,3,36,5,38,7,40,9,..., dimensions={0}, use_global_device_ids=true | all-gather | bytes 530944 | tf_op jit(solution)/shard_map/all_gather | solution.py:186
  45.4 2.6 %all-gather.1 = bf16[32,32,488]{2,1,0:T(8,128)(2,1)S(1)} all-gather(bf16[16,32,488]{2,1,0:T(8,128)(2,1)S(1)} %bitcast.12), channel_id=3, replica_groups=mesh['x'=4,'yl'=2,'c'=2,'yh'=2,'z'=16] {'c'}, dimensions={0}, use_global_device_ids=true | all-gather | bytes 1499136 | tf_op jit(solution)/shard_map/all_gather | solution.py:187
  47.9 0.0 all-to-all-done.tmpl_ref
  47.9 2.7 %gram.1 = f32[2,136,128]{2,1,0:T(8,128)S(1)} custom-call(bf16[2,16,32,488]{3,2,1,0:T(8,128)(2,1)S(1)} %bitcast.8, bf16[16,80,512]{2,1,0:T(8,128)(2,1)S(1)} %all-to-all-done.tmpl_ref), custom_call_target="tpu_custom_call" | custom-call | tf_op jit(solution)/shard_map/gram/pallas_call | solution.py:188
  50.6 2.0 %all-gather.2 = f32[4,136,128]{2,1,0:T(8,128)S(1)} all-gather(f32[2,136,128]{2,1,0:T(8,128)S(1)} %gram.1), channel_id=4, replica_groups=mesh['x'=4,'yl'=2,'c'=2,'yh'=2,'z'=16] {'c'}, dimensions={0}, use_global_device_ids=true | all-gather | bytes 417792 | tf_op jit(solution)/shard_map/all_gather | solution.py:200
  52.6 1.5 %fit.1 = f32[32,8]{1,0:T(8,128)S(1)} custom-call(f32[2,2,136,128]{3,2,1,0:T(8,128)S(1)} %bitcast.9), custom_call_target="tpu_custom_call" | custom-call | tf_op jit(solution)/shard_map/fit/pallas_call | solution.py:201
  54.2 19.1 %all_to_all.16 = f32[32,1,8]{2,1,0:T(1,128)S(1)} all-to-all(f32[32,1,8]{2,1,0:T(1,128)S(1)} %bitcast.10), channel_id=1, replica_groups=mesh['x'=4,'yl'=2,'c'=2,'yh'=2,'z'=16] {'c','z'}, dimensions={0} | all-to-all | bytes 2048 | tf_op jit(solution)/shard_map/all_to_all | solution.py:209
  73.2 0.7 drop.1
Async XLA Ops:
  2.8 45.1 %all-to-all-start = ((bf16[16,80,512]{2,1,0:T(8,128)(2,1)}), bf16[16,80,512]{2,1,0:T(8,128)(2,1)S(1)}, u32[]{:S(2)}, u32[]{:S(2)}) async-start(bf16[16,80,512]{2,1,0:T(8,128)(2,1)} %get-tuple-element.10), calls=%async_computation | async-start | bytes 2621440 | tf_op jit(solution)/shard_map/all_to_all | solution.py:183

commit v5 on v4

--- a/solution.py
+++ b/solution.py
@@ -94,62 +94,55 @@
         )
         split = npairs * 2 * slab
         if s == 0:
-            acc[0:split, :] = gram
-            acc[split:, :] = proj
+            acc[0:split, 0 : 2 * nz] = gram
+            acc[split:, 0 : 2 * nz] = proj
         else:
-            acc[0:split, :] += gram
-            acc[split:, :] += proj
-    entries = npairs + count
-    ntarget = acc.shape[1]
+            acc[0:split, 0 : 2 * nz] += gram
+            acc[split:, 0 : 2 * nz] += proj
+    ntarget = 2 * nz
     fold = LANES // ntarget
+    where = lax.broadcasted_iota(jnp.int32, (slab, LANES), 1) // ntarget
     for h in range(2):
         for g in range(out_ref.shape[1] // slab):
-            parts = []
-            for e in range(g * fold, (g + 1) * fold):
-                at = (2 * min(e, entries - 1) + h) * slab
-                parts.append(acc[at : at + slab, :])
-            out_ref[h, g * slab : (g + 1) * slab, :] = jnp.concatenate(parts, axis=1)
+            packed = None
+            for q in range(fold):
+                e = min(g * fold + q, npairs + count - 1)
+                value = acc[(2 * e + h) * slab : (2 * e + h + 1) * slab, :]
+                if q:
+                    value = pltpu.roll(value, q * ntarget, 1)
+                packed = value if q == 0 else jnp.where(where == q, value, packed)
+            out_ref[h, g * slab : (g + 1) * slab, :] = packed
 
 
 def fit_kernel(part_ref, fit_ref, *, slab, count):
-    npairs = count * (count + 1) // 2
     core = lax.axis_index("c")
     ntarget = fit_ref.shape[0]
     fold = LANES // ntarget
     sums = {}
 
     def entry(e):
-        g = e // fold
+        g, q = divmod(e, fold)
         if g not in sums:
             at = pl.ds(g * slab, slab)
             sums[g] = part_ref[0, core, at, :] + part_ref[1, core, at, :]
-        at = e % fold * ntarget
-        return sums[g][:, at : at + ntarget]
-
-    where = {}
+        return pltpu.roll(sums[g], LANES - q * ntarget, 1) if q else sums[g]
+
+    gram = {}
     for k in range(count):
         for l in range(k, count):
-            where[k, l] = len(where)
-    lower = {}
+            gram[l, k] = entry(len(gram))
+    proj = [entry(len(gram) + k) for k in range(count)]
     fit = None
-    solved = []
     for j in range(count):
-        total = entry(where[j, j])
-        for m in range(j):
-            total = total - lower[j, m] * lower[j, m]
-        inv = lax.rsqrt(total)
+        inv = lax.rsqrt(gram[j, j])
+        column = {i: gram[i, j] * inv for i in range(j + 1, count)}
+        solved = proj[j] * inv
+        fit = solved * solved if fit is None else fit + solved * solved
         for i in range(j + 1, count):
-            value = entry(where[j, i])
-            for m in range(j):
-                value = value - lower[i, m] * lower[j, m]
-            lower[i, j] = value * inv
-        value = entry(npairs + j)
-        for m in range(j):
-            value = value - lower[j, m] * solved[m]
-        value = value * inv
-        solved.append(value)
-        fit = value * value if fit is None else fit + value * value
-    fit_ref[...] = (fit / count).T
+            for m in range(j + 1, i + 1):
+                gram[i, m] = gram[i, m] - column[i] * column[m]
+            proj[i] = proj[i] - column[i] * solved
+    fit_ref[...] = (fit / count).T[0:ntarget, :]
 
 
 def drop_kernel(keep_ref, surface_ref, out_ref):
@@ -192,7 +185,7 @@
         out_specs=VMEM,
         scratch_shapes=[
             pltpu.VMEM((PAD // LANES, 2 * nz * 2 * chunks, LANES), F32),
-            pltpu.VMEM((entries * 2 * slab, 2 * nz), F32),
+            pltpu.VMEM((entries * 2 * slab, LANES), F32),
         ],
         compiler_params=pltpu.CompilerParams(vmem_limit_bytes=16 << 20),
         name="gram",

time: 75.3 us -> 74 us (0.983)
  Pallas kernels: 7.03 us -> 5.74 us
    pallas_call x1, Pallas kernels: 1.52 us -> 0.22 us  [body(): pl.pallas_call(functools.partial(fit_kernel, slab=slab, count=count), out...]
where the time goes in v5:
time: 74 us; the launch traced here: 72.6 us
  blocking collectives  56.8 us (77%)
  starting transfers between devices  9.42 us (13%)
  Pallas kernels  5.74 us (8%)
    all_gather x1, blocking collectives, body(): lax.all_gather(rmsg, ('c', 'z'), axis=0, axis_index_groups=rings)  33.1 us
    all_to_all x1, blocking collectives, body(): surface = lax.all_to_all(fit, ('c', 'z'), 0, 0, tiled=True)  19.1 us
    all_to_all x1, starting transfers between devices, body(): tmpl_all = lax.all_to_all(tmsg, PLANE, 0, 0, tiled=True)  9.42 us
    pallas_call x1, Pallas kernels, body(): pl.pallas_call(functools.partial(gram_kernel, slab=slab, count=count), ou...  2.68 us
    all_gather x1, blocking collectives, body(): rows_all = lax.all_gather(ring_rows, 'c', axis=0)  2.57 us
    pallas_call x1, Pallas kernels, body(): pl.pallas_call(functools.partial(prep_kernel, galaxy_z=total_z * 3 // 10)...  2.17 us
    all_gather x1, blocking collectives, body(): both = lax.all_gather(part, 'c', axis=0)  2.02 us
  transfers between devices with their start and end apart: 1, of which 0 were waited for; matrix products, arithmetic and copies ran while one was open for 0% of the time, Pallas kernels for 0%

profile of v5, /device:TPU:6, one launch (start us, length us, event | category | flops | bytes accessed | tf_op | source)
XLA Modules:
  0.0 72.6 jit_solution(17441586766641802536)
XLA Ops:
  0.7 2.2 %prep.1 = (bf16[32,488]{1,0:T(8,128)(2,1)S(1)}, bf16[16,80,512]{2,1,0:T(8,128)(2,1)}, f32[1,256]{1,0:T(1,128)S(1)}) custom-call(s32[1]{0:T(128)S(6)} %copy.6.classes_ref, bf16[1,7808]{1,0:T(2,128)(2,1)} %flux_ref.1, bf16[1,7808]{1,0:T(2,128)(2,1)} %ivar_ref.1, bf16[10,8,488]{2,1,0:T(8,128)(2,1)} %bitcast.13), custom_call_target="tpu_custom_call" | custom-call | tf_op jit(solution)/shard_map/prep/pallas_call | solution.py:163
  2.8 9.4 %all-to-all-start = ((bf16[16,80,512]{2,1,0:T(8,128)(2,1)}), bf16[16,80,512]{2,1,0:T(8,128)(2,1)S(1)}, u32[]{:S(2)}, u32[]{:S(2)}) async-start(bf16[16,80,512]{2,1,0:T(8,128)(2,1)} %get-tuple-element.10), calls=%async_computation | async-start | bytes 2621440 | tf_op jit(solution)/shard_map/all_to_all | solution.py:176
  12.2 33.1 %all-gather = bf16[512,488]{1,0:T(8,128)(2,1)S(1)} all-gather(bf16[32,488]{1,0:T(8,128)(2,1)S(1)} %get-tuple-element.9), channel_id=2, replica_groups={{0,33,2,35,4,37,6,39,8,41,10,43,12,45,14,47},{32,1,34,3,36,5,38,7,40,9,..., dimensions={0}, use_global_device_ids=true | all-gather | bytes 530944 | tf_op jit(solution)/shard_map/all_gather | solution.py:179
  45.4 2.6 %all-gather.1 = bf16[32,32,488]{2,1,0:T(8,128)(2,1)S(1)} all-gather(bf16[16,32,488]{2,1,0:T(8,128)(2,1)S(1)} %bitcast.12), channel_id=3, replica_groups=mesh['x'=4,'yl'=2,'c'=2,'yh'=2,'z'=16] {'c'}, dimensions={0}, use_global_device_ids=true | all-gather | bytes 1499136 | tf_op jit(solution)/shard_map/all_gather | solution.py:180
  47.9 0.0 all-to-all-done.tmpl_ref
  47.9 2.7 %gram.1 = f32[2,136,128]{2,1,0:T(8,128)S(1)} custom-call(bf16[2,16,32,488]{3,2,1,0:T(8,128)(2,1)S(1)} %bitcast.8, bf16[16,80,512]{2,1,0:T(8,128)(2,1)S(1)} %all-to-all-done.tmpl_ref), custom_call_target="tpu_custom_call" | custom-call | tf_op jit(solution)/shard_map/gram/pallas_call | solution.py:181
  50.6 2.0 %all-gather.2 = f32[4,136,128]{2,1,0:T(8,128)S(1)} all-gather(f32[2,136,128]{2,1,0:T(8,128)S(1)} %gram.1), channel_id=4, replica_groups=mesh['x'=4,'yl'=2,'c'=2,'yh'=2,'z'=16] {'c'}, dimensions={0}, use_global_device_ids=true | all-gather | bytes 417792 | tf_op jit(solution)/shard_map/all_gather | solution.py:193
  52.6 0.2 fit.1
  52.9 19.1 %all_to_all.16 = f32[32,1,8]{2,1,0:T(1,128)S(1)} all-to-all(f32[32,1,8]{2,1,0:T(1,128)S(1)} %bitcast.10), channel_id=1, replica_groups=mesh['x'=4,'yl'=2,'c'=2,'yh'=2,'z'=16] {'c','z'}, dimensions={0} | all-to-all | bytes 2048 | tf_op jit(solution)/shard_map/all_to_all | solution.py:202
  71.9 0.7 drop.1
Async XLA Ops:
  2.8 45.1 %all-to-all-start = ((bf16[16,80,512]{2,1,0:T(8,128)(2,1)}), bf16[16,80,512]{2,1,0:T(8,128)(2,1)S(1)}, u32[]{:S(2)}, u32[]{:S(2)}) async-start(bf16[16,80,512]{2,1,0:T(8,128)(2,1)} %get-tuple-element.10), calls=%async_computation | async-start | bytes 2621440 | tf_op jit(solution)/shard_map/all_to_all | solution.py:176

commit v6 on v5

--- a/solution.py
+++ b/solution.py
@@ -44,7 +44,7 @@
                 row = (core * 2 + which) * chunks + s
                 start = (2 * s + core) * width
                 rows[row : row + 1, :] = value[:, start : start + width]
-    rmsg_ref[...] = rows[...].astype(BF16)
+    rmsg_ref[...] = rows[0 : 4 * chunks, :].astype(BF16)
     zeros = jnp.zeros((count * slab, PAD - width), BF16)
     tile = jnp.concatenate([tmpl_ref[...].reshape(count * slab, width), zeros], axis=1)
     for copy in range(tmsg_ref.shape[0]):
@@ -53,65 +53,57 @@
     keep_ref[...] = jnp.where((zindex < galaxy_z) | (classes_ref[0] == 1), 1.0, 0.0)
 
 
-def gram_kernel(rows_ref, tmpl_ref, out_ref, rows, acc, *, slab, count):
+def gram_kernel(rows_ref, tmpl_ref, out_ref, ivars, weights, *, slab, count):
     chunks = tmpl_ref.shape[0] // 2
     per = 2 * chunks
     nz, width = rows_ref.shape[1], rows_ref.shape[3]
-    npairs = count * (count + 1) // 2
     core, z = lax.axis_index("c"), lax.axis_index("z")
     last = PAD // LANES - 1
-    rows[last] = jnp.zeros_like(rows[last])
+    for ref in (ivars, weights):
+        ref[last] = jnp.zeros_like(ref[last])
     for j in range(2):
         for other in range(nz):
             block = rows_ref[j, other, pl.ds(core * per, per), :].astype(F32)
             owner = lax.rem(j + z + other, 2)
-            at = pl.ds((owner * nz + other) * per, per)
-            for i in range(last + 1):
-                part = block[:, i * LANES : min((i + 1) * LANES, width)]
-                rows[i, at, 0 : part.shape[1]] = part
-    for s in range(chunks):
-        stat = []
-        for which in range(2):
-            value = strided(rows, which * chunks + s, 2 * nz, per)
-            stat.append(value.astype(BF16))
-        tk = []
-        for k in range(count):
-            halves = [
-                tmpl_ref[2 * s + h, k * slab : (k + 1) * slab, :] for h in range(2)
-            ]
-            tk.append(jnp.concatenate(halves, axis=0))
-        pairs = []
-        for k in range(count):
-            for l in range(k, count):
-                pairs.append(
-                    (tk[k].astype(F32) * tk[l].astype(F32)).astype(BF16)
-                )
-        gram = lax.dot_general(
-            jnp.concatenate(pairs, axis=0), stat[0], NT, preferred_element_type=F32
+            at = pl.ds((owner * nz + other) * chunks, chunks)
+            for which, ref in enumerate((ivars, weights)):
+                part = block[which * chunks : (which + 1) * chunks]
+                for i in range(last + 1):
+                    piece = part[:, i * LANES : min((i + 1) * LANES, width)]
+                    ref[i, at, 0 : piece.shape[1]] = piece
+
+    def by_chunk(ref):
+        parts = [strided(ref, s, 2 * nz, chunks).astype(BF16) for s in range(chunks)]
+        return jnp.concatenate(parts, axis=1)
+
+    def template(k):
+        at = slice(k * slab, (k + 1) * slab)
+        parts = [
+            jnp.concatenate([tmpl_ref[2 * s, at, :], tmpl_ref[2 * s + 1, at, :]], axis=0)
+            for s in range(chunks)
+        ]
+        return jnp.concatenate(parts, axis=1)
+
+    def sums(lhs, rhs):
+        out = lax.dot_general(
+            jnp.concatenate(lhs, axis=0), rhs, NT, preferred_element_type=F32
         )
-        proj = lax.dot_general(
-            jnp.concatenate(tk, axis=0), stat[1], NT, preferred_element_type=F32
-        )
-        split = npairs * 2 * slab
-        if s == 0:
-            acc[0:split, 0 : 2 * nz] = gram
-            acc[split:, 0 : 2 * nz] = proj
-        else:
-            acc[0:split, 0 : 2 * nz] += gram
-            acc[split:, 0 : 2 * nz] += proj
-    ntarget = 2 * nz
-    fold = LANES // ntarget
-    where = lax.broadcasted_iota(jnp.int32, (slab, LANES), 1) // ntarget
+        return [out[i * 2 * slab : (i + 1) * 2 * slab] for i in range(len(lhs))]
+
+    stat = by_chunk(ivars)
+    tk = [template(k) for k in range(count)]
+    entries = []
+    for k in range(count):
+        entries += sums([tk[k] * tk[l] for l in range(k, count)], stat)
+    entries += sums(tk, by_chunk(weights))
+    fold = LANES // (2 * nz)
     for h in range(2):
         for g in range(out_ref.shape[1] // slab):
-            packed = None
-            for q in range(fold):
-                e = min(g * fold + q, npairs + count - 1)
-                value = acc[(2 * e + h) * slab : (2 * e + h + 1) * slab, :]
-                if q:
-                    value = pltpu.roll(value, q * ntarget, 1)
-                packed = value if q == 0 else jnp.where(where == q, value, packed)
-            out_ref[h, g * slab : (g + 1) * slab, :] = packed
+            parts = [
+                entries[min(e, len(entries) - 1)][h * slab : (h + 1) * slab]
+                for e in range(g * fold, (g + 1) * fold)
+            ]
+            out_ref[h, g * slab : (g + 1) * slab, :] = jnp.concatenate(parts, axis=1)
 
 
 def fit_kernel(part_ref, fit_ref, *, slab, count):
@@ -169,7 +161,7 @@
         ),
         in_specs=[SMEM] + [VMEM] * 3,
         out_specs=(VMEM, VMEM, VMEM),
-        scratch_shapes=[pltpu.VMEM((4 * chunks, width), F32)],
+        scratch_shapes=[pltpu.VMEM((4 * chunks + 8, width), F32)],
         compiler_params=pltpu.CompilerParams(vmem_limit_bytes=8 << 20),
         name="prep",
     )(classes, in_hbm(flux), in_hbm(ivar), in_hbm(jnp.transpose(templates, (1, 0, 2))))
@@ -184,10 +176,10 @@
         in_specs=[VMEM] * 2,
         out_specs=VMEM,
         scratch_shapes=[
-            pltpu.VMEM((PAD // LANES, 2 * nz * 2 * chunks, LANES), F32),
-            pltpu.VMEM((entries * 2 * slab, LANES), F32),
+            pltpu.VMEM((PAD // LANES, (2 * nz + 1) * chunks, LANES), F32),
+            pltpu.VMEM((PAD // LANES, (2 * nz + 1) * chunks, LANES), F32),
         ],
-        compiler_params=pltpu.CompilerParams(vmem_limit_bytes=16 << 20),
+        compiler_params=pltpu.CompilerParams(vmem_limit_bytes=24 << 20),
         name="gram",
     )(in_vmem(rows_all), tmpl_all)
     both = lax.all_gather(part, "c", axis=0)

time: 74 us -> 73.8 us (level)
  no operation moved by 1% of the time
where the time goes in v6:
time: 73.8 us; the launch traced here: 72.5 us
  blocking collectives  56.8 us (77%)
  starting transfers between devices  9.42 us (13%)
  Pallas kernels  5.6 us (8%)
    all_gather x1, blocking collectives, body(): lax.all_gather(rmsg, ('c', 'z'), axis=0, axis_index_groups=rings)  33.1 us
    all_to_all x1, blocking collectives, body(): surface = lax.all_to_all(fit, ('c', 'z'), 0, 0, tiled=True)  19.1 us
    all_to_all x1, starting transfers between devices, body(): tmpl_all = lax.all_to_all(tmsg, PLANE, 0, 0, tiled=True)  9.42 us
    all_gather x1, blocking collectives, body(): rows_all = lax.all_gather(ring_rows, 'c', axis=0)  2.57 us
    pallas_call x1, Pallas kernels, body(): pl.pallas_call(functools.partial(gram_kernel, slab=slab, count=count), ou...  2.55 us
    pallas_call x1, Pallas kernels, body(): pl.pallas_call(functools.partial(prep_kernel, galaxy_z=total_z * 3 // 10)...  2.17 us
    all_gather x1, blocking collectives, body(): both = lax.all_gather(part, 'c', axis=0)  2.02 us
  transfers between devices with their start and end apart: 1, of which 0 were waited for; matrix products, arithmetic and copies ran while one was open for 0% of the time, Pallas kernels for 0%

profile of v6, /device:TPU:6, one launch (start us, length us, event | category | flops | bytes accessed | tf_op | source)
XLA Modules:
  0.0 72.5 jit_solution(5438473720513888100)
XLA Ops:
  0.7 2.2 %prep.1 = (bf16[32,488]{1,0:T(8,128)(2,1)S(1)}, bf16[16,80,512]{2,1,0:T(8,128)(2,1)}, f32[1,256]{1,0:T(1,128)S(1)}) custom-call(s32[1]{0:T(128)S(6)} %copy.6.classes_ref, bf16[1,7808]{1,0:T(2,128)(2,1)} %flux_ref.1, bf16[1,7808]{1,0:T(2,128)(2,1)} %ivar_ref.1, bf16[10,8,488]{2,1,0:T(8,128)(2,1)} %bitcast.13), custom_call_target="tpu_custom_call" | custom-call | tf_op jit(solution)/shard_map/prep/pallas_call | solution.py:155
  2.8 9.4 %all-to-all-start = ((bf16[16,80,512]{2,1,0:T(8,128)(2,1)}), bf16[16,80,512]{2,1,0:T(8,128)(2,1)S(1)}, u32[]{:S(2)}, u32[]{:S(2)}) async-start(bf16[16,80,512]{2,1,0:T(8,128)(2,1)} %get-tuple-element.10), calls=%async_computation | async-start | bytes 2621440 | tf_op jit(solution)/shard_map/all_to_all | solution.py:168
  12.2 33.1 %all-gather = bf16[512,488]{1,0:T(8,128)(2,1)S(1)} all-gather(bf16[32,488]{1,0:T(8,128)(2,1)S(1)} %get-tuple-element.9), channel_id=2, replica_groups={{0,33,2,35,4,37,6,39,8,41,10,43,12,45,14,47},{32,1,34,3,36,5,38,7,40,9,..., dimensions={0}, use_global_device_ids=true | all-gather | bytes 530944 | tf_op jit(solution)/shard_map/all_gather | solution.py:171
  45.4 2.6 %all-gather.1 = bf16[32,32,488]{2,1,0:T(8,128)(2,1)S(1)} all-gather(bf16[16,32,488]{2,1,0:T(8,128)(2,1)S(1)} %bitcast.12), channel_id=3, replica_groups=mesh['x'=4,'yl'=2,'c'=2,'yh'=2,'z'=16] {'c'}, dimensions={0}, use_global_device_ids=true | all-gather | bytes 1499136 | tf_op jit(solution)/shard_map/all_gather | solution.py:172
  47.9 0.0 all-to-all-done.tmpl_ref
  47.9 2.5 %gram.1 = f32[2,136,128]{2,1,0:T(8,128)S(1)} custom-call(bf16[2,16,32,488]{3,2,1,0:T(8,128)(2,1)S(1)} %bitcast.8, bf16[16,80,512]{2,1,0:T(8,128)(2,1)S(1)} %all-to-all-done.tmpl_ref), custom_call_target="tpu_custom_call" | custom-call | tf_op jit(solution)/shard_map/gram/pallas_call | solution.py:173
  50.5 2.0 %all-gather.2 = f32[4,136,128]{2,1,0:T(8,128)S(1)} all-gather(f32[2,136,128]{2,1,0:T(8,128)S(1)} %gram.1), channel_id=4, replica_groups=mesh['x'=4,'yl'=2,'c'=2,'yh'=2,'z'=16] {'c'}, dimensions={0}, use_global_device_ids=true | all-gather | bytes 417792 | tf_op jit(solution)/shard_map/all_gather | solution.py:185
  52.5 0.2 fit.1
  52.7 19.1 %all_to_all.16 = f32[32,1,8]{2,1,0:T(1,128)S(1)} all-to-all(f32[32,1,8]{2,1,0:T(1,128)S(1)} %bitcast.10), channel_id=1, replica_groups=mesh['x'=4,'yl'=2,'c'=2,'yh'=2,'z'=16] {'c','z'}, dimensions={0} | all-to-all | bytes 2048 | tf_op jit(solution)/shard_map/all_to_all | solution.py:194
  71.8 0.7 drop.1
Async XLA Ops:
  2.8 45.1 %all-to-all-start = ((bf16[16,80,512]{2,1,0:T(8,128)(2,1)}), bf16[16,80,512]{2,1,0:T(8,128)(2,1)S(1)}, u32[]{:S(2)}, u32[]{:S(2)}) async-start(bf16[16,80,512]{2,1,0:T(8,128)(2,1)} %get-tuple-element.10), calls=%async_computation | async-start | bytes 2621440 | tf_op jit(solution)/shard_map/all_to_all | solution.py:168

commit v7 on v6

--- a/solution.py
+++ b/solution.py
@@ -33,20 +33,31 @@
     return jnp.concatenate(parts, axis=1)
 
 
-def prep_kernel(classes_ref, flux_ref, ivar_ref, tmpl_ref, rmsg_ref, tmsg_ref, keep_ref, rows, *, galaxy_z):
-    count, slab, width = tmpl_ref.shape
-    chunks = rmsg_ref.shape[0] // 4
+def pack_kernel(flux_ref, ivar_ref, tmpl_ref, pack_ref, rows):
+    nrows = pack_ref.shape[0] - tmpl_ref.shape[0]
+    width = tmpl_ref.shape[1]
+    chunks = nrows // 4
     ivar = ivar_ref[...].astype(F32)
     weighted = (ivar * flux_ref[...].astype(F32)).astype(BF16).astype(F32)
-    for core in range(2):
+    for half in range(2):
         for which, value in enumerate((ivar, weighted)):
             for s in range(chunks):
-                row = (core * 2 + which) * chunks + s
-                start = (2 * s + core) * width
+                row = (half * 2 + which) * chunks + s
+                start = (2 * s + half) * width
                 rows[row : row + 1, :] = value[:, start : start + width]
-    rmsg_ref[...] = rows[0 : 4 * chunks, :].astype(BF16)
-    zeros = jnp.zeros((count * slab, PAD - width), BF16)
-    tile = jnp.concatenate([tmpl_ref[...].reshape(count * slab, width), zeros], axis=1)
+    pack_ref[0:nrows, :] = rows[0:nrows, :].astype(BF16)
+    pack_ref[nrows:, :] = tmpl_ref[...]
+
+
+def send_kernel(classes_ref, both_ref, rmsg_ref, tmsg_ref, keep_ref, *, galaxy_z):
+    nrows, width = rmsg_ref.shape
+    per = nrows // 2
+    ring = lax.rem(lax.axis_index("c") + lax.axis_index("z"), 2)
+    for core in range(2):
+        rmsg_ref[core * per : (core + 1) * per, :] = both_ref[core, pl.ds(ring * per, per), :]
+    tmpl = both_ref[ring, nrows:, :]
+    zeros = jnp.zeros((tmpl.shape[0], PAD - width), BF16)
+    tile = jnp.concatenate([tmpl, zeros], axis=1)
     for copy in range(tmsg_ref.shape[0]):
         tmsg_ref[copy] = tile
     zindex = lax.broadcasted_iota(jnp.int32, keep_ref.shape, 1)
@@ -55,22 +66,19 @@
 
 def gram_kernel(rows_ref, tmpl_ref, out_ref, ivars, weights, *, slab, count):
     chunks = tmpl_ref.shape[0] // 2
-    per = 2 * chunks
-    nz, width = rows_ref.shape[1], rows_ref.shape[3]
-    core, z = lax.axis_index("c"), lax.axis_index("z")
+    nz, width = rows_ref.shape[0], rows_ref.shape[2]
     last = PAD // LANES - 1
     for ref in (ivars, weights):
         ref[last] = jnp.zeros_like(ref[last])
-    for j in range(2):
-        for other in range(nz):
-            block = rows_ref[j, other, pl.ds(core * per, per), :].astype(F32)
-            owner = lax.rem(j + z + other, 2)
-            at = pl.ds((owner * nz + other) * chunks, chunks)
+    for other in range(nz):
+        block = rows_ref[other].astype(F32)
+        for core in range(2):
             for which, ref in enumerate((ivars, weights)):
-                part = block[which * chunks : (which + 1) * chunks]
+                part = block[(core * 2 + which) * chunks :][:chunks]
+                at = (core * nz + other) * chunks
                 for i in range(last + 1):
                     piece = part[:, i * LANES : min((i + 1) * LANES, width)]
-                    ref[i, at, 0 : piece.shape[1]] = piece
+                    ref[i, at : at + chunks, 0 : piece.shape[1]] = piece
 
     def by_chunk(ref):
         parts = [strided(ref, s, 2 * nz, chunks).astype(BF16) for s in range(chunks)]
@@ -152,24 +160,37 @@
     total_z = lax.axis_size(GZ) * slab
     fold = LANES // (2 * lax.axis_size("z"))
     groups = -(-entries // fold)
+    nrows = 4 * chunks
+    pack = pl.pallas_call(
+        pack_kernel,
+        out_shape=pltpu.VMEM((nrows + count * slab, width), BF16),
+        in_specs=[VMEM] * 3,
+        out_specs=VMEM,
+        scratch_shapes=[pltpu.VMEM((nrows + 8, width), F32)],
+        compiler_params=pltpu.CompilerParams(vmem_limit_bytes=8 << 20),
+        name="pack",
+    )(
+        in_hbm(flux),
+        in_hbm(ivar),
+        in_hbm(jnp.transpose(templates, (1, 0, 2)).reshape(count * slab, width)),
+    )
+    both = lax.all_gather(pack, "c", axis=0)
     rmsg, tmsg, keep = pl.pallas_call(
-        functools.partial(prep_kernel, galaxy_z=total_z * 3 // 10),
+        functools.partial(send_kernel, galaxy_z=total_z * 3 // 10),
         out_shape=(
-            pltpu.VMEM((2 * 2 * chunks, width), BF16),
-            pltpu.VMEM((2 * chunks, count * slab, PAD), BF16),
-            jax.ShapeDtypeStruct((1, total_z), F32),
+            pltpu.VMEM((nrows, width), BF16),
+            jax.ShapeDtypeStruct((2 * chunks, count * slab, PAD), BF16),
+            pltpu.VMEM((1, total_z), F32),
         ),
-        in_specs=[SMEM] + [VMEM] * 3,
+        in_specs=[SMEM, VMEM],
         out_specs=(VMEM, VMEM, VMEM),
-        scratch_shapes=[pltpu.VMEM((4 * chunks + 8, width), F32)],
         compiler_params=pltpu.CompilerParams(vmem_limit_bytes=8 << 20),
-        name="prep",
-    )(classes, in_hbm(flux), in_hbm(ivar), in_hbm(jnp.transpose(templates, (1, 0, 2))))
+        name="send",
+    )(classes, in_vmem(both))
     tmpl_all = lax.all_to_all(tmsg, PLANE, 0, 0, tiled=True)
     nz = lax.axis_size("z")
     rings = [[(g + z) % 2 * nz + z for z in range(nz)] for g in range(2)]
-    ring_rows = lax.all_gather(rmsg, ("c", "z"), axis=0, axis_index_groups=rings)
-    rows_all = lax.all_gather(ring_rows, "c", axis=0)
+    rows_all = lax.all_gather(rmsg, ("c", "z"), axis=0, axis_index_groups=rings)
     part = pl.pallas_call(
         functools.partial(gram_kernel, slab=slab, count=count),
         out_shape=pltpu.VMEM((2, groups * slab, LANES), F32),

time: 73.8 us -> 73.7 us (level)
    pallas_call x1 -> x2, Pallas kernels: 2.17 us -> 2.27 us  [the longest x1 1.2 us: body(): pl.pallas_call(functools.partial(send_kernel, galaxy_z=total_z * 3 // 10)...]
where the time goes in v7:
time: 73.7 us; the launch traced here: 72.4 us
  blocking collectives  56.7 us (77%)
  starting transfers between devices  9.42 us (13%)
  Pallas kernels  5.66 us (8%)
    all_gather x1, blocking collectives, body(): rows_all = lax.all_gather(rmsg, ('c', 'z'), axis=0, axis_index_groups=rings)  33.3 us
    all_to_all x1, blocking collectives, body(): surface = lax.all_to_all(fit, ('c', 'z'), 0, 0, tiled=True)  19.4 us
    all_to_all x1, starting transfers between devices, body(): tmpl_all = lax.all_to_all(tmsg, PLANE, 0, 0, tiled=True)  9.42 us
    pallas_call x1, Pallas kernels, body(): pl.pallas_call(functools.partial(gram_kernel, slab=slab, count=count), ou...  2.5 us
    all_gather x1, blocking collectives, body(): both = lax.all_gather(part, 'c', axis=0)  2.01 us
    all_gather x1, blocking collectives, body(): both = lax.all_gather(pack, 'c', axis=0)  1.97 us
  transfers between devices with their start and end apart: 1, of which 0 were waited for; matrix products, arithmetic and copies ran while one was open for 0% of the time, Pallas kernels for 0%

profile of v7, /device:TPU:6, one launch (start us, length us, event | category | flops | bytes accessed | tf_op | source)
XLA Modules:
  0.0 72.4 jit_solution(3855596966959744600)
XLA Ops:
  0.7 1.1 %pack.1 = bf16[112,488]{1,0:T(8,128)(2,1)S(1)} custom-call(bf16[1,7808]{1,0:T(2,128)(2,1)} %flux_ref.1, bf16[1,7808]{1,0:T(2,128)(2,1)} %ivar_ref.1, bf16[80,488]{1,0:T(8,128)(2,1)} %bitcast.15), custom_call_target="tpu_custom_call" | custom-call | tf_op jit(solution)/shard_map/pack/pallas_call | solution.py:164
  1.7 2.0 %all-gather = bf16[224,488]{1,0:T(8,128)(2,1)S(1)} all-gather(bf16[112,488]{1,0:T(8,128)(2,1)S(1)} %pack.1), channel_id=2, replica_groups=mesh['x'=4,'yl'=2,'c'=2,'yh'=2,'z'=16] {'c'}, dimensions={0}, use_global_device_ids=true | all-gather | bytes 327936 | tf_op jit(solution)/shard_map/all_gather | solution.py:177
  3.7 1.2 %send.1 = (bf16[32,488]{1,0:T(8,128)(2,1)S(1)}, bf16[16,80,512]{2,1,0:T(8,128)(2,1)}, f32[1,256]{1,0:T(1,128)S(1)}) custom-call(s32[1]{0:T(128)S(6)} %copy.6.classes_ref, bf16[2,112,488]{2,1,0:T(8,128)(2,1)S(1)} %bitcast.12), custom_call_target="tpu_custom_call" | custom-call | tf_op jit(solution)/shard_map/send/pallas_call | solution.py:178
  4.9 9.4 %all-to-all-start = ((bf16[16,80,512]{2,1,0:T(8,128)(2,1)}), bf16[16,80,512]{2,1,0:T(8,128)(2,1)S(1)}, u32[]{:S(2)}, u32[]{:S(2)}) async-start(bf16[16,80,512]{2,1,0:T(8,128)(2,1)} %get-tuple-element.10), calls=%async_computation | async-start | bytes 2621440 | tf_op jit(solution)/shard_map/all_to_all | solution.py:190
  14.3 33.3 %all-gather.1 = bf16[512,488]{1,0:T(8,128)(2,1)S(1)} all-gather(bf16[32,488]{1,0:T(8,128)(2,1)S(1)} %get-tuple-element.9), channel_id=3, replica_groups={{0,33,2,35,4,37,6,39,8,41,10,43,12,45,14,47},{32,1,34,3,36,5,38,7,40,9,..., dimensions={0}, use_global_device_ids=true | all-gather | bytes 530944 | tf_op jit(solution)/shard_map/all_gather | solution.py:193
  47.6 0.0 all-to-all-done.tmpl_ref
  47.6 2.5 %gram.1 = f32[2,136,128]{2,1,0:T(8,128)S(1)} custom-call(bf16[16,32,488]{2,1,0:T(8,128)(2,1)S(1)} %bitcast.10, bf16[16,80,512]{2,1,0:T(8,128)(2,1)S(1)} %all-to-all-done.tmpl_ref), custom_call_target="tpu_custom_call" | custom-call | tf_op jit(solution)/shard_map/gram/pallas_call | solution.py:194
  50.1 2.0 %all-gather.2 = f32[4,136,128]{2,1,0:T(8,128)S(1)} all-gather(f32[2,136,128]{2,1,0:T(8,128)S(1)} %gram.1), channel_id=4, replica_groups=mesh['x'=4,'yl'=2,'c'=2,'yh'=2,'z'=16] {'c'}, dimensions={0}, use_global_device_ids=true | all-gather | bytes 417792 | tf_op jit(solution)/shard_map/all_gather | solution.py:206
  52.1 0.2 fit.1
  52.4 19.4 %all_to_all.16 = f32[32,1,8]{2,1,0:T(1,128)S(1)} all-to-all(f32[32,1,8]{2,1,0:T(1,128)S(1)} %bitcast.13), channel_id=1, replica_groups=mesh['x'=4,'yl'=2,'c'=2,'yh'=2,'z'=16] {'c','z'}, dimensions={0} | all-to-all | bytes 2048 | tf_op jit(solution)/shard_map/all_to_all | solution.py:215
  71.7 0.7 drop.1
Async XLA Ops:
  4.9 42.7 %all-to-all-start = ((bf16[16,80,512]{2,1,0:T(8,128)(2,1)}), bf16[16,80,512]{2,1,0:T(8,128)(2,1)S(1)}, u32[]{:S(2)}, u32[]{:S(2)}) async-start(bf16[16,80,512]{2,1,0:T(8,128)(2,1)} %get-tuple-element.10), calls=%async_computation | async-start | bytes 2621440 | tf_op jit(solution)/shard_map/all_to_all | solution.py:190

commit v8 on v7

--- a/solution.py
+++ b/solution.py
@@ -75,7 +75,7 @@
         for core in range(2):
             for which, ref in enumerate((ivars, weights)):
                 part = block[(core * 2 + which) * chunks :][:chunks]
-                at = (core * nz + other) * chunks
+                at = ((core + other) % 2 * nz + other) * chunks
                 for i in range(last + 1):
                     piece = part[:, i * LANES : min((i + 1) * LANES, width)]
                     ref[i, at : at + chunks, 0 : piece.shape[1]] = piece
@@ -104,27 +104,29 @@
     for k in range(count):
         entries += sums([tk[k] * tk[l] for l in range(k, count)], stat)
     entries += sums(tk, by_chunk(weights))
-    fold = LANES // (2 * nz)
-    for h in range(2):
-        for g in range(out_ref.shape[1] // slab):
+    fold = LANES // nz
+    for ring in range(2):
+        lanes = slice(ring * nz, (ring + 1) * nz)
+        for g in range(out_ref.shape[1] // (2 * slab)):
             parts = [
-                entries[min(e, len(entries) - 1)][h * slab : (h + 1) * slab]
+                entries[min(e, len(entries) - 1)][:, lanes]
                 for e in range(g * fold, (g + 1) * fold)
             ]
-            out_ref[h, g * slab : (g + 1) * slab, :] = jnp.concatenate(parts, axis=1)
-
-
-def fit_kernel(part_ref, fit_ref, *, slab, count):
-    core = lax.axis_index("c")
-    ntarget = fit_ref.shape[0]
+            at = slice(g * 2 * slab, (g + 1) * 2 * slab)
+            out_ref[ring, at, :] = jnp.concatenate(parts, axis=1)
+
+
+def fit_kernel(part_ref, fit_ref, *, count):
+    ring = lax.rem(lax.axis_index("c") + lax.axis_index("z"), 2)
+    ntarget, rows = fit_ref.shape
     fold = LANES // ntarget
     sums = {}
 
     def entry(e):
         g, q = divmod(e, fold)
         if g not in sums:
-            at = pl.ds(g * slab, slab)
-            sums[g] = part_ref[0, core, at, :] + part_ref[1, core, at, :]
+            at = pl.ds(g * rows, rows)
+            sums[g] = part_ref[0, ring, at, :] + part_ref[1, ring, at, :]
         return pltpu.roll(sums[g], LANES - q * ntarget, 1) if q else sums[g]
 
     gram = {}
@@ -146,11 +148,13 @@
 
 
 def drop_kernel(keep_ref, surface_ref, out_ref):
-    nsrc, slab = surface_ref.shape
-    for i in range(nsrc):
-        at = slice(i * slab, (i + 1) * slab)
-        value = surface_ref[i : i + 1, :]
-        out_ref[:, at] = jnp.where(keep_ref[:, at] > 0.0, value, 0.0)
+    nz, rows = surface_ref.shape
+    slab = rows // 2
+    for half in range(2):
+        for z in range(nz):
+            at = slice((half * nz + z) * slab, (half * nz + z + 1) * slab)
+            value = surface_ref[z : z + 1, half * slab : (half + 1) * slab]
+            out_ref[:, at] = jnp.where(keep_ref[:, at] > 0.0, value, 0.0)
 
 
 def body(flux, ivar, templates, classes):
@@ -158,7 +162,7 @@
     entries = count * (count + 1) // 2 + count
     chunks = flux.shape[1] // width // 2
     total_z = lax.axis_size(GZ) * slab
-    fold = LANES // (2 * lax.axis_size("z"))
+    fold = LANES // lax.axis_size("z")
     groups = -(-entries // fold)
     nrows = 4 * chunks
     pack = pl.pallas_call(
@@ -193,7 +197,7 @@
     rows_all = lax.all_gather(rmsg, ("c", "z"), axis=0, axis_index_groups=rings)
     part = pl.pallas_call(
         functools.partial(gram_kernel, slab=slab, count=count),
-        out_shape=pltpu.VMEM((2, groups * slab, LANES), F32),
+        out_shape=pltpu.VMEM((2, groups * 2 * slab, LANES), F32),
         in_specs=[VMEM] * 2,
         out_specs=VMEM,
         scratch_shapes=[
@@ -205,14 +209,16 @@
     )(in_vmem(rows_all), tmpl_all)
     both = lax.all_gather(part, "c", axis=0)
     fit = pl.pallas_call(
-        functools.partial(fit_kernel, slab=slab, count=count),
-        out_shape=pltpu.VMEM((2 * nz, slab), F32),
+        functools.partial(fit_kernel, count=count),
+        out_shape=pltpu.VMEM((nz, 2 * slab), F32),
         in_specs=[VMEM],
         out_specs=VMEM,
         compiler_params=pltpu.CompilerParams(vmem_limit_bytes=4 << 20),
         name="fit",
     )(in_vmem(both))
-    surface = lax.all_to_all(fit, ("c", "z"), 0, 0, tiled=True)
+    surface = lax.all_to_all(
+        fit, ("c", "z"), 0, 0, tiled=True, axis_index_groups=rings
+    )
     return pl.pallas_call(
         drop_kernel,
         out_shape=jax.ShapeDtypeStruct((1, total_z), F32),

time: 73.7 us -> 72.8 us (0.988); the launches traced: 72.4 us -> 72.4 us
  no operation moved by 1% of the time
where the time goes in v8:
time: 72.8 us; the launch traced here: 72.4 us
  blocking collectives  56.6 us (78%)
  starting transfers between devices  9.42 us (13%)
  Pallas kernels  5.75 us (8%)
    all_gather x1, blocking collectives, body(): rows_all = lax.all_gather(rmsg, ('c', 'z'), axis=0, axis_index_groups=rings)  33.3 us
    all_to_all x1, blocking collectives, body(): lax.all_to_all(fit, ('c', 'z'), 0, 0, tiled=True, axis_index_groups=rings)  19.3 us
    all_to_all x1, starting transfers between devices, body(): tmpl_all = lax.all_to_all(tmsg, PLANE, 0, 0, tiled=True)  9.42 us
    pallas_call x1, Pallas kernels, body(): pl.pallas_call(functools.partial(gram_kernel, slab=slab, count=count), ou...  2.52 us
    all_gather x1, blocking collectives, body(): both = lax.all_gather(part, 'c', axis=0)  2.02 us
    all_gather x1, blocking collectives, body(): both = lax.all_gather(pack, 'c', axis=0)  1.97 us
  transfers between devices with their start and end apart: 1, of which 0 were waited for; matrix products, arithmetic and copies ran while one was open for 0% of the time, Pallas kernels for 0%

profile of v8, /device:TPU:6, one launch (start us, length us, event | category | flops | bytes accessed | tf_op | source)
XLA Modules:
  0.0 72.4 jit_solution(11640510750603813507)
XLA Ops:
  0.7 1.1 %pack.1 = bf16[112,488]{1,0:T(8,128)(2,1)S(1)} custom-call(bf16[1,7808]{1,0:T(2,128)(2,1)} %flux_ref.1, bf16[1,7808]{1,0:T(2,128)(2,1)} %ivar_ref.1, bf16[80,488]{1,0:T(8,128)(2,1)} %bitcast.15), custom_call_target="tpu_custom_call" | custom-call | tf_op jit(solution)/shard_map/pack/pallas_call | solution.py:168
  1.7 2.0 %all-gather = bf16[224,488]{1,0:T(8,128)(2,1)S(1)} all-gather(bf16[112,488]{1,0:T(8,128)(2,1)S(1)} %pack.1), channel_id=2, replica_groups=mesh['x'=4,'yl'=2,'c'=2,'yh'=2,'z'=16] {'c'}, dimensions={0}, use_global_device_ids=true | all-gather | bytes 327936 | tf_op jit(solution)/shard_map/all_gather | solution.py:181
  3.7 1.2 %send.1 = (bf16[32,488]{1,0:T(8,128)(2,1)S(1)}, bf16[16,80,512]{2,1,0:T(8,128)(2,1)}, f32[1,256]{1,0:T(1,128)S(1)}) custom-call(s32[1]{0:T(128)S(6)} %copy.6.classes_ref, bf16[2,112,488]{2,1,0:T(8,128)(2,1)S(1)} %bitcast.12), custom_call_target="tpu_custom_call" | custom-call | tf_op jit(solution)/shard_map/send/pallas_call | solution.py:182
  4.9 9.4 %all-to-all-start = ((bf16[16,80,512]{2,1,0:T(8,128)(2,1)}), bf16[16,80,512]{2,1,0:T(8,128)(2,1)S(1)}, u32[]{:S(2)}, u32[]{:S(2)}) async-start(bf16[16,80,512]{2,1,0:T(8,128)(2,1)} %get-tuple-element.10), calls=%async_computation | async-start | bytes 2621440 | tf_op jit(solution)/shard_map/all_to_all | solution.py:194
  14.3 33.3 %all-gather.1 = bf16[512,488]{1,0:T(8,128)(2,1)S(1)} all-gather(bf16[32,488]{1,0:T(8,128)(2,1)S(1)} %get-tuple-element.9), channel_id=3, replica_groups={{0,33,2,35,4,37,6,39,8,41,10,43,12,45,14,47},{32,1,34,3,36,5,38,7,40,9,..., dimensions={0}, use_global_device_ids=true | all-gather | bytes 530944 | tf_op jit(solution)/shard_map/all_gather | solution.py:197
  47.6 0.0 all-to-all-done.tmpl_ref
  47.6 2.5 %gram.1 = f32[2,144,128]{2,1,0:T(8,128)S(1)} custom-call(bf16[16,32,488]{2,1,0:T(8,128)(2,1)S(1)} %bitcast.10, bf16[16,80,512]{2,1,0:T(8,128)(2,1)S(1)} %all-to-all-done.tmpl_ref), custom_call_target="tpu_custom_call" | custom-call | tf_op jit(solution)/shard_map/gram/pallas_call | solution.py:198
  50.2 2.0 %all-gather.2 = f32[4,144,128]{2,1,0:T(8,128)S(1)} all-gather(f32[2,144,128]{2,1,0:T(8,128)S(1)} %gram.1), channel_id=4, replica_groups=mesh['x'=4,'yl'=2,'c'=2,'yh'=2,'z'=16] {'c'}, dimensions={0}, use_global_device_ids=true | all-gather | bytes 442368 | tf_op jit(solution)/shard_map/all_gather | solution.py:210
  52.2 0.3 fit.1
  52.5 19.3 %all_to_all.16 = f32[16,1,16]{2,1,0:T(1,128)S(1)} all-to-all(f32[16,1,16]{2,1,0:T(1,128)S(1)} %bitcast.13), channel_id=1, replica_groups={{0,33,2,35,4,37,6,39,8,41,10,43,12,45,14,47},{32,1,34,3,36,5,38,7,40,9,..., dimensions={0} | all-to-all | bytes 2048 | tf_op jit(solution)/shard_map/all_to_all | solution.py:219
  71.8 0.7 drop.1
Async XLA Ops:
  4.9 42.7 %all-to-all-start = ((bf16[16,80,512]{2,1,0:T(8,128)(2,1)}), bf16[16,80,512]{2,1,0:T(8,128)(2,1)S(1)}, u32[]{:S(2)}, u32[]{:S(2)}) async-start(bf16[16,80,512]{2,1,0:T(8,128)(2,1)} %get-tuple-element.10), calls=%async_computation | async-start | bytes 2621440 | tf_op jit(solution)/shard_map/all_to_all | solution.py:194

commit v9 on v8

--- a/solution.py
+++ b/solution.py
@@ -92,48 +92,42 @@
         ]
         return jnp.concatenate(parts, axis=1)
 
-    def sums(lhs, rhs):
+    tk = [template(k) for k in range(count)]
+    pairs = [tk[k] * tk[l] for k in range(count) for l in range(k, count)]
+    fold = LANES // (2 * slab)
+    at = 0
+    for lhs, rhs in ((by_chunk(ivars), pairs), (by_chunk(weights), tk)):
+        zeros = [jnp.zeros_like(tk[0])] * (-len(rhs) % fold)
         out = lax.dot_general(
-            jnp.concatenate(lhs, axis=0), rhs, NT, preferred_element_type=F32
+            lhs, jnp.concatenate(rhs + zeros, axis=0), NT, preferred_element_type=F32
         )
-        return [out[i * 2 * slab : (i + 1) * 2 * slab] for i in range(len(lhs))]
-
-    stat = by_chunk(ivars)
-    tk = [template(k) for k in range(count)]
-    entries = []
-    for k in range(count):
-        entries += sums([tk[k] * tk[l] for l in range(k, count)], stat)
-    entries += sums(tk, by_chunk(weights))
-    fold = LANES // nz
-    for ring in range(2):
-        lanes = slice(ring * nz, (ring + 1) * nz)
-        for g in range(out_ref.shape[1] // (2 * slab)):
-            parts = [
-                entries[min(e, len(entries) - 1)][:, lanes]
-                for e in range(g * fold, (g + 1) * fold)
-            ]
-            at = slice(g * 2 * slab, (g + 1) * 2 * slab)
-            out_ref[ring, at, :] = jnp.concatenate(parts, axis=1)
+        for g in range(out.shape[1] // LANES):
+            for ring in range(2):
+                value = out[ring * nz : (ring + 1) * nz, g * LANES : (g + 1) * LANES]
+                out_ref[ring, at : at + nz, :] = value
+            at += nz
 
 
 def fit_kernel(part_ref, fit_ref, *, count):
     ring = lax.rem(lax.axis_index("c") + lax.axis_index("z"), 2)
-    ntarget, rows = fit_ref.shape
-    fold = LANES // ntarget
+    ntarget, width = fit_ref.shape
+    fold = LANES // width
+    npairs = count * (count + 1) // 2
+    first_proj = -(-npairs // fold) * fold
     sums = {}
 
     def entry(e):
         g, q = divmod(e, fold)
         if g not in sums:
-            at = pl.ds(g * rows, rows)
+            at = pl.ds(g * ntarget, ntarget)
             sums[g] = part_ref[0, ring, at, :] + part_ref[1, ring, at, :]
-        return pltpu.roll(sums[g], LANES - q * ntarget, 1) if q else sums[g]
+        return pltpu.roll(sums[g], LANES - q * width, 1) if q else sums[g]
 
     gram = {}
     for k in range(count):
         for l in range(k, count):
             gram[l, k] = entry(len(gram))
-    proj = [entry(len(gram) + k) for k in range(count)]
+    proj = [entry(first_proj + k) for k in range(count)]
     fit = None
     for j in range(count):
         inv = lax.rsqrt(gram[j, j])
@@ -144,7 +138,7 @@
             for m in range(j + 1, i + 1):
                 gram[i, m] = gram[i, m] - column[i] * column[m]
             proj[i] = proj[i] - column[i] * solved
-    fit_ref[...] = (fit / count).T[0:ntarget, :]
+    fit_ref[...] = (fit / count)[:, 0:width]
 
 
 def drop_kernel(keep_ref, surface_ref, out_ref):
@@ -159,11 +153,10 @@
 
 def body(flux, ivar, templates, classes):
     slab, count, width = templates.shape
-    entries = count * (count + 1) // 2 + count
     chunks = flux.shape[1] // width // 2
     total_z = lax.axis_size(GZ) * slab
-    fold = LANES // lax.axis_size("z")
-    groups = -(-entries // fold)
+    fold = LANES // (2 * slab)
+    groups = -(-(count * (count + 1) // 2) // fold) + -(-count // fold)
     nrows = 4 * chunks
     pack = pl.pallas_call(
         pack_kernel,
@@ -197,7 +190,7 @@
     rows_all = lax.all_gather(rmsg, ("c", "z"), axis=0, axis_index_groups=rings)
     part = pl.pallas_call(
         functools.partial(gram_kernel, slab=slab, count=count),
-        out_shape=pltpu.VMEM((2, groups * 2 * slab, LANES), F32),
+        out_shape=pltpu.VMEM((2, groups * lax.axis_size("z"), LANES), F32),
         in_specs=[VMEM] * 2,
         out_specs=VMEM,
         scratch_shapes=[

time: 72.8 us -> 72.7 us (level)
  no operation moved by 1% of the time
where the time goes in v9:
time: 72.7 us; the launch traced here: 72.4 us
  blocking collectives  56.6 us (78%)
  starting transfers between devices  9.42 us (13%)
  Pallas kernels  5.69 us (8%)
    all_gather x1, blocking collectives, body(): rows_all = lax.all_gather(rmsg, ('c', 'z'), axis=0, axis_index_groups=rings)  33.3 us
    all_to_all x1, blocking collectives, body(): lax.all_to_all(fit, ('c', 'z'), 0, 0, tiled=True, axis_index_groups=rings)  19.3 us
    all_to_all x1, starting transfers between devices, body(): tmpl_all = lax.all_to_all(tmsg, PLANE, 0, 0, tiled=True)  9.42 us
    pallas_call x1, Pallas kernels, body(): pl.pallas_call(functools.partial(gram_kernel, slab=slab, count=count), ou...  2.53 us
    all_gather x1, blocking collectives, body(): both = lax.all_gather(part, 'c', axis=0)  2.02 us
    all_gather x1, blocking collectives, body(): both = lax.all_gather(pack, 'c', axis=0)  1.97 us
  transfers between devices with their start and end apart: 1, of which 0 were waited for; matrix products, arithmetic and copies ran while one was open for 0% of the time, Pallas kernels for 0%

profile of v9, /device:TPU:6, one launch (start us, length us, event | category | flops | bytes accessed | tf_op | source)
XLA Modules:
  0.0 72.4 jit_solution(1564422606657286264)
XLA Ops:
  0.7 1.1 %pack.1 = bf16[112,488]{1,0:T(8,128)(2,1)S(1)} custom-call(bf16[1,7808]{1,0:T(2,128)(2,1)} %flux_ref.1, bf16[1,7808]{1,0:T(2,128)(2,1)} %ivar_ref.1, bf16[80,488]{1,0:T(8,128)(2,1)} %bitcast.15), custom_call_target="tpu_custom_call" | custom-call | tf_op jit(solution)/shard_map/pack/pallas_call | solution.py:161
  1.7 2.0 %all-gather = bf16[224,488]{1,0:T(8,128)(2,1)S(1)} all-gather(bf16[112,488]{1,0:T(8,128)(2,1)S(1)} %pack.1), channel_id=2, replica_groups=mesh['x'=4,'yl'=2,'c'=2,'yh'=2,'z'=16] {'c'}, dimensions={0}, use_global_device_ids=true | all-gather | bytes 327936 | tf_op jit(solution)/shard_map/all_gather | solution.py:174
  3.7 1.2 %send.1 = (bf16[32,488]{1,0:T(8,128)(2,1)S(1)}, bf16[16,80,512]{2,1,0:T(8,128)(2,1)}, f32[1,256]{1,0:T(1,128)S(1)}) custom-call(s32[1]{0:T(128)S(6)} %copy.6.classes_ref, bf16[2,112,488]{2,1,0:T(8,128)(2,1)S(1)} %bitcast.12), custom_call_target="tpu_custom_call" | custom-call | tf_op jit(solution)/shard_map/send/pallas_call | solution.py:175
  4.9 9.4 %all-to-all-start = ((bf16[16,80,512]{2,1,0:T(8,128)(2,1)}), bf16[16,80,512]{2,1,0:T(8,128)(2,1)S(1)}, u32[]{:S(2)}, u32[]{:S(2)}) async-start(bf16[16,80,512]{2,1,0:T(8,128)(2,1)} %get-tuple-element.10), calls=%async_computation | async-start | bytes 2621440 | tf_op jit(solution)/shard_map/all_to_all | solution.py:187
  14.3 33.3 %all-gather.1 = bf16[512,488]{1,0:T(8,128)(2,1)S(1)} all-gather(bf16[32,488]{1,0:T(8,128)(2,1)S(1)} %get-tuple-element.9), channel_id=3, replica_groups={{0,33,2,35,4,37,6,39,8,41,10,43,12,45,14,47},{32,1,34,3,36,5,38,7,40,9,..., dimensions={0}, use_global_device_ids=true | all-gather | bytes 530944 | tf_op jit(solution)/shard_map/all_gather | solution.py:190
  47.6 0.0 all-to-all-done.tmpl_ref
  47.6 2.5 %gram.1 = f32[2,144,128]{2,1,0:T(8,128)S(1)} custom-call(bf16[16,32,488]{2,1,0:T(8,128)(2,1)S(1)} %bitcast.10, bf16[16,80,512]{2,1,0:T(8,128)(2,1)S(1)} %all-to-all-done.tmpl_ref), custom_call_target="tpu_custom_call" | custom-call | tf_op jit(solution)/shard_map/gram/pallas_call | solution.py:191
  50.2 2.0 %all-gather.2 = f32[4,144,128]{2,1,0:T(8,128)S(1)} all-gather(f32[2,144,128]{2,1,0:T(8,128)S(1)} %gram.1), channel_id=4, replica_groups=mesh['x'=4,'yl'=2,'c'=2,'yh'=2,'z'=16] {'c'}, dimensions={0}, use_global_device_ids=true | all-gather | bytes 442368 | tf_op jit(solution)/shard_map/all_gather | solution.py:203
  52.2 0.2 fit.1
  52.4 19.3 %all_to_all.16 = f32[16,1,16]{2,1,0:T(1,128)S(1)} all-to-all(f32[16,1,16]{2,1,0:T(1,128)S(1)} %bitcast.13), channel_id=1, replica_groups={{0,33,2,35,4,37,6,39,8,41,10,43,12,45,14,47},{32,1,34,3,36,5,38,7,40,9,..., dimensions={0} | all-to-all | bytes 2048 | tf_op jit(solution)/shard_map/all_to_all | solution.py:212
  71.7 0.7 drop.1
Async XLA Ops:
  4.9 42.7 %all-to-all-start = ((bf16[16,80,512]{2,1,0:T(8,128)(2,1)}), bf16[16,80,512]{2,1,0:T(8,128)(2,1)S(1)}, u32[]{:S(2)}, u32[]{:S(2)}) async-start(bf16[16,80,512]{2,1,0:T(8,128)(2,1)} %get-tuple-element.10), calls=%async_computation | async-start | bytes 2621440 | tf_op jit(solution)/shard_map/all_to_all | solution.py:187

commit v10 on v9

--- a/solution.py
+++ b/solution.py
@@ -64,7 +64,7 @@
     keep_ref[...] = jnp.where((zindex < galaxy_z) | (classes_ref[0] == 1), 1.0, 0.0)
 
 
-def gram_kernel(rows_ref, tmpl_ref, out_ref, ivars, weights, *, slab, count):
+def gram_kernel(rows_ref, tmpl_ref, own_ref, other_ref, ivars, weights, *, slab, count):
     chunks = tmpl_ref.shape[0] // 2
     nz, width = rows_ref.shape[0], rows_ref.shape[2]
     last = PAD // LANES - 1
@@ -94,6 +94,7 @@
 
     tk = [template(k) for k in range(count)]
     pairs = [tk[k] * tk[l] for k in range(count) for l in range(k, count)]
+    first = lax.rem(lax.axis_index("c") + lax.axis_index("z"), 2) == 0
     fold = LANES // (2 * slab)
     at = 0
     for lhs, rhs in ((by_chunk(ivars), pairs), (by_chunk(weights), tk)):
@@ -102,14 +103,15 @@
             lhs, jnp.concatenate(rhs + zeros, axis=0), NT, preferred_element_type=F32
         )
         for g in range(out.shape[1] // LANES):
-            for ring in range(2):
-                value = out[ring * nz : (ring + 1) * nz, g * LANES : (g + 1) * LANES]
-                out_ref[ring, at : at + nz, :] = value
+            lanes = slice(g * LANES, (g + 1) * LANES)
+            low, high = out[0:nz, lanes], out[nz : 2 * nz, lanes]
+            own_ref[at : at + nz, :] = jnp.where(first, low, high)
+            other_ref[at : at + nz, :] = jnp.where(first, high, low)
             at += nz
 
 
-def fit_kernel(part_ref, fit_ref, *, count):
-    ring = lax.rem(lax.axis_index("c") + lax.axis_index("z"), 2)
+def fit_kernel(own_ref, sent_ref, fit_ref, *, count):
+    partner = 1 - lax.axis_index("c")
     ntarget, width = fit_ref.shape
     fold = LANES // width
     npairs = count * (count + 1) // 2
@@ -120,7 +122,7 @@
         g, q = divmod(e, fold)
         if g not in sums:
             at = pl.ds(g * ntarget, ntarget)
-            sums[g] = part_ref[0, ring, at, :] + part_ref[1, ring, at, :]
+            sums[g] = own_ref[at, :] + sent_ref[partner, at, :]
         return pltpu.roll(sums[g], LANES - q * width, 1) if q else sums[g]
 
     gram = {}
@@ -188,11 +190,11 @@
     nz = lax.axis_size("z")
     rings = [[(g + z) % 2 * nz + z for z in range(nz)] for g in range(2)]
     rows_all = lax.all_gather(rmsg, ("c", "z"), axis=0, axis_index_groups=rings)
-    part = pl.pallas_call(
+    own, other = pl.pallas_call(
         functools.partial(gram_kernel, slab=slab, count=count),
-        out_shape=pltpu.VMEM((2, groups * lax.axis_size("z"), LANES), F32),
+        out_shape=(pltpu.VMEM((groups * nz, LANES), F32),) * 2,
         in_specs=[VMEM] * 2,
-        out_specs=VMEM,
+        out_specs=(VMEM, VMEM),
         scratch_shapes=[
             pltpu.VMEM((PAD // LANES, (2 * nz + 1) * chunks, LANES), F32),
             pltpu.VMEM((PAD // LANES, (2 * nz + 1) * chunks, LANES), F32),
@@ -200,15 +202,15 @@
         compiler_params=pltpu.CompilerParams(vmem_limit_bytes=24 << 20),
         name="gram",
     )(in_vmem(rows_all), tmpl_all)
-    both = lax.all_gather(part, "c", axis=0)
+    sent = lax.all_gather(other, "c", axis=0)
     fit = pl.pallas_call(
         functools.partial(fit_kernel, count=count),
         out_shape=pltpu.VMEM((nz, 2 * slab), F32),
-        in_specs=[VMEM],
+        in_specs=[VMEM, VMEM],
         out_specs=VMEM,
         compiler_params=pltpu.CompilerParams(vmem_limit_bytes=4 << 20),
         name="fit",
-    )(in_vmem(both))
+    )(in_vmem(own), in_vmem(sent))
     surface = lax.all_to_all(
         fit, ("c", "z"), 0, 0, tiled=True, axis_index_groups=rings
     )

time: 72.7 us -> 72.6 us (level)
  no operation moved by 1% of the time
where the time goes in v10:
time: 72.6 us; the launch traced here: 72.3 us
  blocking collectives  56.5 us (78%)
  starting transfers between devices  9.42 us (13%)
  Pallas kernels  5.69 us (8%)
    all_gather x1, blocking collectives, body(): rows_all = lax.all_gather(rmsg, ('c', 'z'), axis=0, axis_index_groups=rings)  33.3 us
    all_to_all x1, blocking collectives, body(): lax.all_to_all(fit, ('c', 'z'), 0, 0, tiled=True, axis_index_groups=rings)  19.3 us
    all_to_all x1, starting transfers between devices, body(): tmpl_all = lax.all_to_all(tmsg, PLANE, 0, 0, tiled=True)  9.42 us
    pallas_call x1, Pallas kernels, body(): pl.pallas_call(functools.partial(gram_kernel, slab=slab, count=count), ou...  2.53 us
    all_gather x1, blocking collectives, body(): both = lax.all_gather(pack, 'c', axis=0)  1.97 us
    all_gather x1, blocking collectives, body(): sent = lax.all_gather(other, 'c', axis=0)  1.91 us
  transfers between devices with their start and end apart: 1, of which 0 were waited for; matrix products, arithmetic and copies ran while one was open for 0% of the time, Pallas kernels for 0%

profile of v10, /device:TPU:6, one launch (start us, length us, event | category | flops | bytes accessed | tf_op | source)
XLA Modules:
  0.0 72.3 jit_solution(2470693058118292192)
XLA Ops:
  0.7 1.1 %pack.1 = bf16[112,488]{1,0:T(8,128)(2,1)S(1)} custom-call(bf16[1,7808]{1,0:T(2,128)(2,1)} %flux_ref.1, bf16[1,7808]{1,0:T(2,128)(2,1)} %ivar_ref.1, bf16[80,488]{1,0:T(8,128)(2,1)} %bitcast.15), custom_call_target="tpu_custom_call" | custom-call | tf_op jit(solution)/shard_map/pack/pallas_call | solution.py:163
  1.7 2.0 %all-gather = bf16[224,488]{1,0:T(8,128)(2,1)S(1)} all-gather(bf16[112,488]{1,0:T(8,128)(2,1)S(1)} %pack.1), channel_id=2, replica_groups=mesh['x'=4,'yl'=2,'c'=2,'yh'=2,'z'=16] {'c'}, dimensions={0}, use_global_device_ids=true | all-gather | bytes 327936 | tf_op jit(solution)/shard_map/all_gather | solution.py:176
  3.7 1.2 %send.1 = (bf16[32,488]{1,0:T(8,128)(2,1)S(1)}, bf16[16,80,512]{2,1,0:T(8,128)(2,1)}, f32[1,256]{1,0:T(1,128)S(1)}) custom-call(s32[1]{0:T(128)S(6)} %copy.6.classes_ref, bf16[2,112,488]{2,1,0:T(8,128)(2,1)S(1)} %bitcast.11), custom_call_target="tpu_custom_call" | custom-call | tf_op jit(solution)/shard_map/send/pallas_call | solution.py:177
  4.9 9.4 %all-to-all-start = ((bf16[16,80,512]{2,1,0:T(8,128)(2,1)}), bf16[16,80,512]{2,1,0:T(8,128)(2,1)S(1)}, u32[]{:S(2)}, u32[]{:S(2)}) async-start(bf16[16,80,512]{2,1,0:T(8,128)(2,1)} %get-tuple-element.12), calls=%async_computation | async-start | bytes 2621440 | tf_op jit(solution)/shard_map/all_to_all | solution.py:189
  14.3 33.3 %all-gather.1 = bf16[512,488]{1,0:T(8,128)(2,1)S(1)} all-gather(bf16[32,488]{1,0:T(8,128)(2,1)S(1)} %get-tuple-element.11), channel_id=3, replica_groups={{0,33,2,35,4,37,6,39,8,41,10,43,12,45,14,47},{32,1,34,3,36,5,38,7,40,9,..., dimensions={0}, use_global_device_ids=true | all-gather | bytes 530944 | tf_op jit(solution)/shard_map/all_gather | solution.py:192
  47.6 0.0 all-to-all-done.tmpl_ref
  47.6 2.5 %gram.1 = (f32[144,128]{1,0:T(8,128)S(1)}, f32[144,128]{1,0:T(8,128)S(1)}) custom-call(bf16[16,32,488]{2,1,0:T(8,128)(2,1)S(1)} %bitcast.10, bf16[16,80,512]{2,1,0:T(8,128)(2,1)S(1)} %all-to-all-done.tmpl_ref), custom_call_target="tpu_custom_call" | custom-call | tf_op jit(solution)/shard_map/gram/pallas_call | solution.py:193
  50.2 1.9 %all-gather.2 = f32[288,128]{1,0:T(8,128)S(1)} all-gather(f32[144,128]{1,0:T(8,128)S(1)} %get-tuple-element.14), channel_id=4, replica_groups=mesh['x'=4,'yl'=2,'c'=2,'yh'=2,'z'=16] {'c'}, dimensions={0}, use_global_device_ids=true | all-gather | bytes 221184 | tf_op jit(solution)/shard_map/all_gather | solution.py:205
  52.1 0.2 fit.1
  52.3 19.3 %all_to_all.16 = f32[16,1,16]{2,1,0:T(1,128)S(1)} all-to-all(f32[16,1,16]{2,1,0:T(1,128)S(1)} %bitcast.13), channel_id=1, replica_groups={{0,33,2,35,4,37,6,39,8,41,10,43,12,45,14,47},{32,1,34,3,36,5,38,7,40,9,..., dimensions={0} | all-to-all | bytes 2048 | tf_op jit(solution)/shard_map/all_to_all | solution.py:214
  71.6 0.7 drop.1
Async XLA Ops:
  4.9 42.7 %all-to-all-start = ((bf16[16,80,512]{2,1,0:T(8,128)(2,1)}), bf16[16,80,512]{2,1,0:T(8,128)(2,1)S(1)}, u32[]{:S(2)}, u32[]{:S(2)}) async-start(bf16[16,80,512]{2,1,0:T(8,128)(2,1)} %get-tuple-element.12), calls=%async_computation | async-start | bytes 2621440 | tf_op jit(solution)/shard_map/all_to_all | solution.py:189

commit v11 on v9

--- a/solution.py
+++ b/solution.py
@@ -138,7 +138,10 @@
             for m in range(j + 1, i + 1):
                 gram[i, m] = gram[i, m] - column[i] * column[m]
             proj[i] = proj[i] - column[i] * solved
-    fit_ref[...] = (fit / count)[:, 0:width]
+    fit = (fit / count)[:, 0:width]
+    middle = ntarget // 2
+    fit_ref[0 : ntarget - middle, :] = fit[middle:, :]
+    fit_ref[ntarget - middle :, :] = fit[0:middle, :]
 
 
 def drop_kernel(keep_ref, surface_ref, out_ref):
@@ -147,7 +150,8 @@
     for half in range(2):
         for z in range(nz):
             at = slice((half * nz + z) * slab, (half * nz + z + 1) * slab)
-            value = surface_ref[z : z + 1, half * slab : (half + 1) * slab]
+            row = (z - nz // 2) % nz
+            value = surface_ref[row : row + 1, half * slab : (half + 1) * slab]
             out_ref[:, at] = jnp.where(keep_ref[:, at] > 0.0, value, 0.0)
 
 
@@ -209,8 +213,9 @@
         compiler_params=pltpu.CompilerParams(vmem_limit_bytes=4 << 20),
         name="fit",
     )(in_vmem(both))
+    turned = [ring[nz // 2 :] + ring[: nz // 2] for ring in rings]
     surface = lax.all_to_all(
-        fit, ("c", "z"), 0, 0, tiled=True, axis_index_groups=rings
+        fit, ("c", "z"), 0, 0, tiled=True, axis_index_groups=turned
     )
     return pl.pallas_call(
         drop_kernel,

time: 72.7 us -> 68.1 us (0.937)
  blocking collectives: 56.6 us -> 51.5 us
    all_to_all x1, blocking collectives: 19.3 us -> 14.2 us  [body(): lax.all_to_all(fit, ('c', 'z'), 0, 0, tiled=True, axis_index_groups=turned)]
where the time goes in v11:
time: 68.1 us; the launch traced here: 67.3 us
  blocking collectives  51.5 us (76%)
  starting transfers between devices  9.42 us (14%)
  Pallas kernels  5.69 us (8%)
    all_gather x1, blocking collectives, body(): rows_all = lax.all_gather(rmsg, ('c', 'z'), axis=0, axis_index_groups=rings)  33.3 us
    all_to_all x1, blocking collectives, body(): lax.all_to_all(fit, ('c', 'z'), 0, 0, tiled=True, axis_index_groups=turned)  14.2 us
    all_to_all x1, starting transfers between devices, body(): tmpl_all = lax.all_to_all(tmsg, PLANE, 0, 0, tiled=True)  9.42 us
    pallas_call x1, Pallas kernels, body(): pl.pallas_call(functools.partial(gram_kernel, slab=slab, count=count), ou...  2.53 us
    all_gather x1, blocking collectives, body(): both = lax.all_gather(part, 'c', axis=0)  2.02 us
    all_gather x1, blocking collectives, body(): both = lax.all_gather(pack, 'c', axis=0)  1.97 us
  transfers between devices with their start and end apart: 1, of which 0 were waited for; matrix products, arithmetic and copies ran while one was open for 0% of the time, Pallas kernels for 0%

profile of v11, /device:TPU:6, one launch (start us, length us, event | category | flops | bytes accessed | tf_op | source)
XLA Modules:
  0.0 67.3 jit_solution(2874187713946609287)
XLA Ops:
  0.7 1.1 %pack.1 = bf16[112,488]{1,0:T(8,128)(2,1)S(1)} custom-call(bf16[1,7808]{1,0:T(2,128)(2,1)} %flux_ref.1, bf16[1,7808]{1,0:T(2,128)(2,1)} %ivar_ref.1, bf16[80,488]{1,0:T(8,128)(2,1)} %bitcast.15), custom_call_target="tpu_custom_call" | custom-call | tf_op jit(solution)/shard_map/pack/pallas_call | solution.py:165
  1.7 2.0 %all-gather = bf16[224,488]{1,0:T(8,128)(2,1)S(1)} all-gather(bf16[112,488]{1,0:T(8,128)(2,1)S(1)} %pack.1), channel_id=2, replica_groups=mesh['x'=4,'yl'=2,'c'=2,'yh'=2,'z'=16] {'c'}, dimensions={0}, use_global_device_ids=true | all-gather | bytes 327936 | tf_op jit(solution)/shard_map/all_gather | solution.py:178
  3.7 1.2 %send.1 = (bf16[32,488]{1,0:T(8,128)(2,1)S(1)}, bf16[16,80,512]{2,1,0:T(8,128)(2,1)}, f32[1,256]{1,0:T(1,128)S(1)}) custom-call(s32[1]{0:T(128)S(6)} %copy.6.classes_ref, bf16[2,112,488]{2,1,0:T(8,128)(2,1)S(1)} %bitcast.12), custom_call_target="tpu_custom_call" | custom-call | tf_op jit(solution)/shard_map/send/pallas_call | solution.py:179
  4.9 9.4 %all-to-all-start = ((bf16[16,80,512]{2,1,0:T(8,128)(2,1)}), bf16[16,80,512]{2,1,0:T(8,128)(2,1)S(1)}, u32[]{:S(2)}, u32[]{:S(2)}) async-start(bf16[16,80,512]{2,1,0:T(8,128)(2,1)} %get-tuple-element.10), calls=%async_computation | async-start | bytes 2621440 | tf_op jit(solution)/shard_map/all_to_all | solution.py:191
  14.3 33.3 %all-gather.1 = bf16[512,488]{1,0:T(8,128)(2,1)S(1)} all-gather(bf16[32,488]{1,0:T(8,128)(2,1)S(1)} %get-tuple-element.9), channel_id=3, replica_groups={{0,33,2,35,4,37,6,39,8,41,10,43,12,45,14,47},{32,1,34,3,36,5,38,7,40,9,..., dimensions={0}, use_global_device_ids=true | all-gather | bytes 530944 | tf_op jit(solution)/shard_map/all_gather | solution.py:194
  47.6 0.0 all-to-all-done.tmpl_ref
  47.6 2.5 %gram.1 = f32[2,144,128]{2,1,0:T(8,128)S(1)} custom-call(bf16[16,32,488]{2,1,0:T(8,128)(2,1)S(1)} %bitcast.10, bf16[16,80,512]{2,1,0:T(8,128)(2,1)S(1)} %all-to-all-done.tmpl_ref), custom_call_target="tpu_custom_call" | custom-call | tf_op jit(solution)/shard_map/gram/pallas_call | solution.py:195
  50.2 2.0 %all-gather.2 = f32[4,144,128]{2,1,0:T(8,128)S(1)} all-gather(f32[2,144,128]{2,1,0:T(8,128)S(1)} %gram.1), channel_id=4, replica_groups=mesh['x'=4,'yl'=2,'c'=2,'yh'=2,'z'=16] {'c'}, dimensions={0}, use_global_device_ids=true | all-gather | bytes 442368 | tf_op jit(solution)/shard_map/all_gather | solution.py:207
  52.2 0.2 fit.1
  52.4 14.2 %all_to_all.16 = f32[16,1,16]{2,1,0:T(1,128)S(1)} all-to-all(f32[16,1,16]{2,1,0:T(1,128)S(1)} %bitcast.13), channel_id=1, replica_groups={{8,41,10,43,12,45,14,47,0,33,2,35,4,37,6,39},{40,9,42,11,44,13,46,15,32..., dimensions={0} | all-to-all | bytes 2048 | tf_op jit(solution)/shard_map/all_to_all | solution.py:217
  66.6 0.7 drop.1
Async XLA Ops:
  4.9 42.7 %all-to-all-start = ((bf16[16,80,512]{2,1,0:T(8,128)(2,1)}), bf16[16,80,512]{2,1,0:T(8,128)(2,1)S(1)}, u32[]{:S(2)}, u32[]{:S(2)}) async-start(bf16[16,80,512]{2,1,0:T(8,128)(2,1)} %get-tuple-element.10), calls=%async_computation | async-start | bytes 2621440 | tf_op jit(solution)/shard_map/all_to_all | solution.py:191

commit v12 on v10

--- a/solution.py
+++ b/solution.py
@@ -140,7 +140,10 @@
             for m in range(j + 1, i + 1):
                 gram[i, m] = gram[i, m] - column[i] * column[m]
             proj[i] = proj[i] - column[i] * solved
-    fit_ref[...] = (fit / count)[:, 0:width]
+    fit = (fit / count)[:, 0:width]
+    middle = ntarget // 2
+    fit_ref[0 : ntarget - middle, :] = fit[middle:, :]
+    fit_ref[ntarget - middle :, :] = fit[0:middle, :]
 
 
 def drop_kernel(keep_ref, surface_ref, out_ref):
@@ -149,7 +152,8 @@
     for half in range(2):
         for z in range(nz):
             at = slice((half * nz + z) * slab, (half * nz + z + 1) * slab)
-            value = surface_ref[z : z + 1, half * slab : (half + 1) * slab]
+            row = (z - nz // 2) % nz
+            value = surface_ref[row : row + 1, half * slab : (half + 1) * slab]
             out_ref[:, at] = jnp.where(keep_ref[:, at] > 0.0, value, 0.0)
 
 
@@ -211,8 +215,9 @@
         compiler_params=pltpu.CompilerParams(vmem_limit_bytes=4 << 20),
         name="fit",
     )(in_vmem(own), in_vmem(sent))
+    turned = [ring[nz // 2 :] + ring[: nz // 2] for ring in rings]
     surface = lax.all_to_all(
-        fit, ("c", "z"), 0, 0, tiled=True, axis_index_groups=rings
+        fit, ("c", "z"), 0, 0, tiled=True, axis_index_groups=turned
     )
     return pl.pallas_call(
         drop_kernel,

time: 72.6 us -> 68 us (0.937)
  blocking collectives: 56.5 us -> 51.4 us
    all_to_all x1, blocking collectives: 19.3 us -> 14.2 us  [body(): lax.all_to_all(fit, ('c', 'z'), 0, 0, tiled=True, axis_index_groups=turned)]
where the time goes in v12:
time: 68 us; the launch traced here: 67.2 us
  blocking collectives  51.4 us (76%)
  starting transfers between devices  9.42 us (14%)
  Pallas kernels  5.69 us (8%)
    all_gather x1, blocking collectives, body(): rows_all = lax.all_gather(rmsg, ('c', 'z'), axis=0, axis_index_groups=rings)  33.3 us
    all_to_all x1, blocking collectives, body(): lax.all_to_all(fit, ('c', 'z'), 0, 0, tiled=True, axis_index_groups=turned)  14.2 us
    all_to_all x1, starting transfers between devices, body(): tmpl_all = lax.all_to_all(tmsg, PLANE, 0, 0, tiled=True)  9.42 us
    pallas_call x1, Pallas kernels, body(): pl.pallas_call(functools.partial(gram_kernel, slab=slab, count=count), ou...  2.53 us
    all_gather x1, blocking collectives, body(): both = lax.all_gather(pack, 'c', axis=0)  1.97 us
    all_gather x1, blocking collectives, body(): sent = lax.all_gather(other, 'c', axis=0)  1.91 us
  transfers between devices with their start and end apart: 1, of which 0 were waited for; matrix products, arithmetic and copies ran while one was open for 0% of the time, Pallas kernels for 0%

profile of v12, /device:TPU:6, one launch (start us, length us, event | category | flops | bytes accessed | tf_op | source)
XLA Modules:
  0.0 67.2 jit_solution(13991659624013860660)
XLA Ops:
  0.7 1.1 %pack.1 = bf16[112,488]{1,0:T(8,128)(2,1)S(1)} custom-call(bf16[1,7808]{1,0:T(2,128)(2,1)} %flux_ref.1, bf16[1,7808]{1,0:T(2,128)(2,1)} %ivar_ref.1, bf16[80,488]{1,0:T(8,128)(2,1)} %bitcast.15), custom_call_target="tpu_custom_call" | custom-call | tf_op jit(solution)/shard_map/pack/pallas_call | solution.py:167
  1.7 2.0 %all-gather = bf16[224,488]{1,0:T(8,128)(2,1)S(1)} all-gather(bf16[112,488]{1,0:T(8,128)(2,1)S(1)} %pack.1), channel_id=2, replica_groups=mesh['x'=4,'yl'=2,'c'=2,'yh'=2,'z'=16] {'c'}, dimensions={0}, use_global_device_ids=true | all-gather | bytes 327936 | tf_op jit(solution)/shard_map/all_gather | solution.py:180
  3.7 1.2 %send.1 = (bf16[32,488]{1,0:T(8,128)(2,1)S(1)}, bf16[16,80,512]{2,1,0:T(8,128)(2,1)}, f32[1,256]{1,0:T(1,128)S(1)}) custom-call(s32[1]{0:T(128)S(6)} %copy.6.classes_ref, bf16[2,112,488]{2,1,0:T(8,128)(2,1)S(1)} %bitcast.11), custom_call_target="tpu_custom_call" | custom-call | tf_op jit(solution)/shard_map/send/pallas_call | solution.py:181
  4.9 9.4 %all-to-all-start = ((bf16[16,80,512]{2,1,0:T(8,128)(2,1)}), bf16[16,80,512]{2,1,0:T(8,128)(2,1)S(1)}, u32[]{:S(2)}, u32[]{:S(2)}) async-start(bf16[16,80,512]{2,1,0:T(8,128)(2,1)} %get-tuple-element.12), calls=%async_computation | async-start | bytes 2621440 | tf_op jit(solution)/shard_map/all_to_all | solution.py:193
  14.3 33.3 %all-gather.1 = bf16[512,488]{1,0:T(8,128)(2,1)S(1)} all-gather(bf16[32,488]{1,0:T(8,128)(2,1)S(1)} %get-tuple-element.11), channel_id=3, replica_groups={{0,33,2,35,4,37,6,39,8,41,10,43,12,45,14,47},{32,1,34,3,36,5,38,7,40,9,..., dimensions={0}, use_global_device_ids=true | all-gather | bytes 530944 | tf_op jit(solution)/shard_map/all_gather | solution.py:196
  47.6 0.0 all-to-all-done.tmpl_ref
  47.6 2.5 %gram.1 = (f32[144,128]{1,0:T(8,128)S(1)}, f32[144,128]{1,0:T(8,128)S(1)}) custom-call(bf16[16,32,488]{2,1,0:T(8,128)(2,1)S(1)} %bitcast.10, bf16[16,80,512]{2,1,0:T(8,128)(2,1)S(1)} %all-to-all-done.tmpl_ref), custom_call_target="tpu_custom_call" | custom-call | tf_op jit(solution)/shard_map/gram/pallas_call | solution.py:197
  50.2 1.9 %all-gather.2 = f32[288,128]{1,0:T(8,128)S(1)} all-gather(f32[144,128]{1,0:T(8,128)S(1)} %get-tuple-element.14), channel_id=4, replica_groups=mesh['x'=4,'yl'=2,'c'=2,'yh'=2,'z'=16] {'c'}, dimensions={0}, use_global_device_ids=true | all-gather | bytes 221184 | tf_op jit(solution)/shard_map/all_gather | solution.py:209
  52.1 0.2 fit.1
  52.3 14.2 %all_to_all.16 = f32[16,1,16]{2,1,0:T(1,128)S(1)} all-to-all(f32[16,1,16]{2,1,0:T(1,128)S(1)} %bitcast.13), channel_id=1, replica_groups={{8,41,10,43,12,45,14,47,0,33,2,35,4,37,6,39},{40,9,42,11,44,13,46,15,32..., dimensions={0} | all-to-all | bytes 2048 | tf_op jit(solution)/shard_map/all_to_all | solution.py:219
  66.5 0.7 drop.1
Async XLA Ops:
  4.9 42.7 %all-to-all-start = ((bf16[16,80,512]{2,1,0:T(8,128)(2,1)}), bf16[16,80,512]{2,1,0:T(8,128)(2,1)S(1)}, u32[]{:S(2)}, u32[]{:S(2)}) async-start(bf16[16,80,512]{2,1,0:T(8,128)(2,1)} %get-tuple-element.12), calls=%async_computation | async-start | bytes 2621440 | tf_op jit(solution)/shard_map/all_to_all | solution.py:193

commit v13 on v12

--- a/solution.py
+++ b/solution.py
@@ -98,15 +98,16 @@
     fold = LANES // (2 * slab)
     at = 0
     for lhs, rhs in ((by_chunk(ivars), pairs), (by_chunk(weights), tk)):
-        zeros = [jnp.zeros_like(tk[0])] * (-len(rhs) % fold)
+        zeros = [jnp.zeros_like(tk[0])] * (len(rhs) % 2)
         out = lax.dot_general(
             lhs, jnp.concatenate(rhs + zeros, axis=0), NT, preferred_element_type=F32
         )
-        for g in range(out.shape[1] // LANES):
-            lanes = slice(g * LANES, (g + 1) * LANES)
+        for g in range(-(-out.shape[1] // LANES)):
+            lanes = slice(g * LANES, min((g + 1) * LANES, out.shape[1]))
+            size = lanes.stop - lanes.start
             low, high = out[0:nz, lanes], out[nz : 2 * nz, lanes]
-            own_ref[at : at + nz, :] = jnp.where(first, low, high)
-            other_ref[at : at + nz, :] = jnp.where(first, high, low)
+            own_ref[at : at + nz, 0:size] = jnp.where(first, low, high)
+            other_ref[at : at + nz, 0:size] = jnp.where(first, high, low)
             at += nz
 
 

time: 68 us -> 68 us (level)
  no operation moved by 1% of the time
where the time goes in v13:
time: 68 us; the launch traced here: 67.2 us
  blocking collectives  51.4 us (76%)
  starting transfers between devices  9.42 us (14%)
  Pallas kernels  5.69 us (8%)
    all_gather x1, blocking collectives, body(): rows_all = lax.all_gather(rmsg, ('c', 'z'), axis=0, axis_index_groups=rings)  33.3 us
    all_to_all x1, blocking collectives, body(): lax.all_to_all(fit, ('c', 'z'), 0, 0, tiled=True, axis_index_groups=turned)  14.2 us
    all_to_all x1, starting transfers between devices, body(): tmpl_all = lax.all_to_all(tmsg, PLANE, 0, 0, tiled=True)  9.42 us
    pallas_call x1, Pallas kernels, body(): pl.pallas_call(functools.partial(gram_kernel, slab=slab, count=count), ou...  2.53 us
    all_gather x1, blocking collectives, body(): both = lax.all_gather(pack, 'c', axis=0)  1.97 us
    all_gather x1, blocking collectives, body(): sent = lax.all_gather(other, 'c', axis=0)  1.91 us
  transfers between devices with their start and end apart: 1, of which 0 were waited for; matrix products, arithmetic and copies ran while one was open for 0% of the time, Pallas kernels for 0%

profile of v13, /device:TPU:6, one launch (start us, length us, event | category | flops | bytes accessed | tf_op | source)
XLA Modules:
  0.0 67.2 jit_solution(14897224397638665626)
XLA Ops:
  0.7 1.1 %pack.1 = bf16[112,488]{1,0:T(8,128)(2,1)S(1)} custom-call(bf16[1,7808]{1,0:T(2,128)(2,1)} %flux_ref.1, bf16[1,7808]{1,0:T(2,128)(2,1)} %ivar_ref.1, bf16[80,488]{1,0:T(8,128)(2,1)} %bitcast.15), custom_call_target="tpu_custom_call" | custom-call | tf_op jit(solution)/shard_map/pack/pallas_call | solution.py:168
  1.7 2.0 %all-gather = bf16[224,488]{1,0:T(8,128)(2,1)S(1)} all-gather(bf16[112,488]{1,0:T(8,128)(2,1)S(1)} %pack.1), channel_id=2, replica_groups=mesh['x'=4,'yl'=2,'c'=2,'yh'=2,'z'=16] {'c'}, dimensions={0}, use_global_device_ids=true | all-gather | bytes 327936 | tf_op jit(solution)/shard_map/all_gather | solution.py:181
  3.7 1.2 %send.1 = (bf16[32,488]{1,0:T(8,128)(2,1)S(1)}, bf16[16,80,512]{2,1,0:T(8,128)(2,1)}, f32[1,256]{1,0:T(1,128)S(1)}) custom-call(s32[1]{0:T(128)S(6)} %copy.6.classes_ref, bf16[2,112,488]{2,1,0:T(8,128)(2,1)S(1)} %bitcast.11), custom_call_target="tpu_custom_call" | custom-call | tf_op jit(solution)/shard_map/send/pallas_call | solution.py:182
  4.9 9.4 %all-to-all-start = ((bf16[16,80,512]{2,1,0:T(8,128)(2,1)}), bf16[16,80,512]{2,1,0:T(8,128)(2,1)S(1)}, u32[]{:S(2)}, u32[]{:S(2)}) async-start(bf16[16,80,512]{2,1,0:T(8,128)(2,1)} %get-tuple-element.12), calls=%async_computation | async-start | bytes 2621440 | tf_op jit(solution)/shard_map/all_to_all | solution.py:194
  14.3 33.3 %all-gather.1 = bf16[512,488]{1,0:T(8,128)(2,1)S(1)} all-gather(bf16[32,488]{1,0:T(8,128)(2,1)S(1)} %get-tuple-element.11), channel_id=3, replica_groups={{0,33,2,35,4,37,6,39,8,41,10,43,12,45,14,47},{32,1,34,3,36,5,38,7,40,9,..., dimensions={0}, use_global_device_ids=true | all-gather | bytes 530944 | tf_op jit(solution)/shard_map/all_gather | solution.py:197
  47.6 0.0 all-to-all-done.tmpl_ref
  47.6 2.5 %gram.1 = (f32[144,128]{1,0:T(8,128)S(1)}, f32[144,128]{1,0:T(8,128)S(1)}) custom-call(bf16[16,32,488]{2,1,0:T(8,128)(2,1)S(1)} %bitcast.10, bf16[16,80,512]{2,1,0:T(8,128)(2,1)S(1)} %all-to-all-done.tmpl_ref), custom_call_target="tpu_custom_call" | custom-call | tf_op jit(solution)/shard_map/gram/pallas_call | solution.py:198
  50.2 1.9 %all-gather.2 = f32[288,128]{1,0:T(8,128)S(1)} all-gather(f32[144,128]{1,0:T(8,128)S(1)} %get-tuple-element.14), channel_id=4, replica_groups=mesh['x'=4,'yl'=2,'c'=2,'yh'=2,'z'=16] {'c'}, dimensions={0}, use_global_device_ids=true | all-gather | bytes 221184 | tf_op jit(solution)/shard_map/all_gather | solution.py:210
  52.1 0.2 fit.1
  52.3 14.2 %all_to_all.16 = f32[16,1,16]{2,1,0:T(1,128)S(1)} all-to-all(f32[16,1,16]{2,1,0:T(1,128)S(1)} %bitcast.13), channel_id=1, replica_groups={{8,41,10,43,12,45,14,47,0,33,2,35,4,37,6,39},{40,9,42,11,44,13,46,15,32..., dimensions={0} | all-to-all | bytes 2048 | tf_op jit(solution)/shard_map/all_to_all | solution.py:220
  66.5 0.7 drop.1
Async XLA Ops:
  4.9 42.7 %all-to-all-start = ((bf16[16,80,512]{2,1,0:T(8,128)(2,1)}), bf16[16,80,512]{2,1,0:T(8,128)(2,1)S(1)}, u32[]{:S(2)}, u32[]{:S(2)}) async-start(bf16[16,80,512]{2,1,0:T(8,128)(2,1)} %get-tuple-element.12), calls=%async_computation | async-start | bytes 2621440 | tf_op jit(solution)/shard_map/all_to_all | solution.py:194
